TPU v7x, 128 devices: a whole 4x4x4 slice. The times are simulated.
128 devices in a mesh: fam: 4 (over z), ctx: 32 (over x, y, core).
Axes of the slice: x: 4, y: 4, z: 4, core: 2. Of those that a mesh axis runs over, the one named last changes fastest.
Arguments:
- queries: bfloat16 [4, 16384, 1024], P('fam', 'ctx'), may hold values from -7 to 7
- key_rows: bfloat16 [4, 16384, 1024], P('fam', 'ctx'), may hold values from -4 to 4
- value_rows: bfloat16 [4, 16384, 1024], P('fam', 'ctx'), may hold values from -6 to 6
- cotangent: bfloat16 [4, 16384, 1024], P('fam', 'ctx'), may hold values from -6 to 6
- out_weight: bfloat16 [1024, 1024], replicated, may hold values from -0.1875 to 0.1875
- prot_blocks: int32 [4, 32], P('fam'), may hold values from 1 to 8, 128 in all within a row
- last_fill: int32 [4, 32], P('fam'), may hold values from 1 to 128
- memory_slots: int32 [4, 512], P('fam'), may hold values from 0 to 511
Outputs:
- query_grad: bfloat16 [4, 16384, 1024], P('fam', 'ctx')
- key_grad: bfloat16 [4, 16384, 1024], P('fam', 'ctx')
- value_grad: bfloat16 [4, 16384, 1024], P('fam', 'ctx')
- weight_grad: float32 [1024, 1024], replicated
Inputs may be any that keep to these rules, and one draw needn't show every extreme that they name: `prot_blocks`: each family's protein lengths, in blocks, sum to 128, and the longest has exactly 8 blocks.
All inputs are finite; a program needn't handle non-finite values.
Results may differ from a plain program's by a relative error of at most 0.015.
Values may be sent and summed in bfloat16 or wider, within the bound.
A program may use at most 128 MiB of HBM per device.

v0:
```python
import jax
import jax.numpy as jnp
from jax import lax
from jax.sharding import PartitionSpec as P

HEAD_DIM = 64
W = 512
BLK = 128


NEG_FILL = -1e30


def passed_along(value, axis, steps):
    count = lax.axis_size(axis)
    initial, last = (max(0, -steps), min(count, count - steps))
    return lax.ppermute(value, axis, [(source, source + steps) for source in range(initial, last)])


def protein_tables(prot_blocks, last_fill):
    prot_ends = jnp.cumsum(prot_blocks)
    starts = prot_ends - prot_blocks
    valid_len = (prot_blocks - 1) * BLK + last_fill
    return (prot_ends, starts, valid_len)


def token_info(positions, tables):
    prot_ends, starts, valid_len = tables
    prot_count = prot_ends.shape[0]
    block_ids = jnp.floor_divide(positions, BLK)
    protein = jnp.sum((block_ids[:, None] >= prot_ends[None, :]).astype(jnp.int32), axis=1)
    onehot = protein[:, None] == jnp.arange(prot_count, dtype=jnp.int32)[None, :]
    first_block = jnp.sum(jnp.where(onehot, starts[None, :], 0), axis=1)
    allowed = jnp.sum(jnp.where(onehot, valid_len[None, :], 0), axis=1)
    is_valid = (positions >= 0) & (protein < prot_count) & (positions - first_block * BLK < allowed)
    return (protein, is_valid)


def band_mask(query_pos, query_info, key_pos, key_info):
    return (
        query_info[1][:, None]
        & key_info[1][None, :]
        & (query_info[0][:, None] == key_info[0][None, :])
        & (key_pos[None, :] <= query_pos[:, None])
        & (query_pos[:, None] - key_pos[None, :] < W)
    )


def columns_of(array, column, span):
    return lax.dynamic_slice_in_dim(array, column, span, 1)


def add_into(target, update, row_start, column):
    row_index = jnp.asarray(row_start, jnp.int32)
    current = lax.dynamic_slice(target, (row_index, column), update.shape)
    return lax.dynamic_update_slice(target, current + update, (row_index, column))


def attend(query_blk, grad_blk, key_blk, value_blk, live_mask):
    scale = HEAD_DIM ** (-0.5)
    scores = (
        jnp.einsum("qge,kge->gqk", query_blk, key_blk, preferred_element_type=jnp.float32) * scale
    )
    live = live_mask[None]
    shifted = jnp.where(live, scores, NEG_FILL)
    row_max = jnp.max(shifted, axis=-1, keepdims=True)
    expo = jnp.where(live, jnp.exp(shifted - row_max), 0.0)
    row_sum = jnp.maximum(jnp.sum(expo, axis=-1, keepdims=True), 1.0)
    attn_prob = expo / row_sum
    prob_half = attn_prob.astype(jnp.bfloat16)
    attended = jnp.einsum(
        "gqk,kge->qge", prob_half, value_blk, preferred_element_type=jnp.float32
    ).astype(jnp.bfloat16)
    grad_prob = jnp.einsum("qge,kge->gqk", grad_blk, value_blk, preferred_element_type=jnp.float32)
    row_dot = jnp.sum(attn_prob * grad_prob, axis=-1, keepdims=True)
    grad_score = (attn_prob * (grad_prob - row_dot) * scale).astype(jnp.bfloat16)
    grad_query = jnp.einsum("gqk,kge->qge", grad_score, key_blk, preferred_element_type=jnp.float32)
    grad_key = jnp.einsum("gqk,qge->kge", grad_score, query_blk, preferred_element_type=jnp.float32)
    grad_value = jnp.einsum("gqk,qge->kge", prob_half, grad_blk, preferred_element_type=jnp.float32)
    return (attended, grad_query, grad_key, grad_value, row_max, row_sum, row_dot)


def per_device(
    queries, key_rows, value_rows, cotangent, out_weight, prot_blocks, last_fill, memory_slots
):
    query_loc = queries[0]
    key_loc = key_rows[0]
    value_loc = value_rows[0]
    grad_out = cotangent[0]
    tables = protein_tables(prot_blocks[0], last_fill[0])
    slots = memory_slots[0]
    tokens, width = query_loc.shape
    span = 2 * HEAD_DIM
    pair_count = width // span
    heads_total = width // HEAD_DIM
    ctx_size = lax.axis_size("ctx")
    ctx_index = lax.axis_index("ctx")
    slot_total = slots.shape[0]
    slot_dev = slot_total // ctx_size
    base = ctx_index * tokens
    positions = base + jnp.arange(tokens, dtype=jnp.int32)
    own_info = token_info(positions, tables)
    ext_pos = base - W + jnp.arange(W + tokens, dtype=jnp.int32)
    ext_info = token_info(ext_pos, tables)
    source = jnp.arange(slot_total, dtype=jnp.int32) // slot_dev * tokens + slots
    mem_info = token_info(source, tables)
    own_slots = lax.dynamic_slice_in_dim(slots, ctx_index * slot_dev, slot_dev)
    mem_keys, mem_values = (
        lax.all_gather(key_loc[own_slots], "ctx", axis=0, tiled=True),
        lax.all_gather(value_loc[own_slots], "ctx", axis=0, tiled=True),
    )
    halo_keys, halo_values = passed_along((key_loc, value_loc), "ctx", 1)
    ext_keys = jnp.concatenate([halo_keys, key_loc], axis=0)
    ext_values = jnp.concatenate([halo_values, value_loc], axis=0)
    grad_attn = jnp.einsum(
        "te,de->td", grad_out, out_weight, preferred_element_type=jnp.float32
    ).astype(jnp.bfloat16)
    masks = []
    query_info = (own_info[0], own_info[1])
    key_info = (ext_info[0], ext_info[1])
    band = band_mask(positions, query_info, ext_pos, key_info)
    memory = (
        query_info[1][:, None]
        & mem_info[1][None, :]
        & (mem_info[0][None, :] < query_info[0][:, None])
    )
    masks.append(jnp.concatenate([band, memory], axis=1))

    def pair_step(head_pair, carry):
        (
            query_grad,
            band_kgrad,
            band_vgrad,
            mem_kgrad,
            mem_vgrad,
            attn_rows,
            stat_max,
            stat_sum,
            stat_dot,
        ) = carry
        column = head_pair * span
        query_pair = columns_of(query_loc, column, span).reshape(tokens, 2, HEAD_DIM)
        dout_pair = columns_of(grad_attn, column, span).reshape(tokens, 2, HEAD_DIM)
        key_band = columns_of(ext_keys, column, span).reshape(W + tokens, 2, HEAD_DIM)
        value_band = columns_of(ext_values, column, span).reshape(W + tokens, 2, HEAD_DIM)
        key_memory = columns_of(mem_keys, column, span).reshape(slot_total, 2, HEAD_DIM)
        value_memory = columns_of(mem_values, column, span).reshape(slot_total, 2, HEAD_DIM)
        key_blk = jnp.concatenate([key_band, key_memory], axis=0)
        value_blk = jnp.concatenate([value_band, value_memory], axis=0)
        attended, grad_query, grad_key, grad_value, row_max, row_sum, row_dot = attend(
            query_pair, dout_pair, key_blk, value_blk, masks[0]
        )
        row_index = jnp.asarray(0, jnp.int32)
        query_grad = lax.dynamic_update_slice(
            query_grad, grad_query.reshape(W, span), (row_index, column)
        )
        attn_rows = lax.dynamic_update_slice(
            attn_rows, attended.reshape(W, span), (row_index, column)
        )
        band_kgrad = add_into(band_kgrad, grad_key[: 2 * W].reshape(2 * W, span), 0, column)
        band_vgrad = add_into(band_vgrad, grad_value[: 2 * W].reshape(2 * W, span), 0, column)
        mem_kgrad = add_into(mem_kgrad, grad_key[2 * W :].reshape(slot_total, span), 0, column)
        mem_vgrad = add_into(mem_vgrad, grad_value[2 * W :].reshape(slot_total, span), 0, column)
        stat_col = head_pair * 2
        zero_row = jnp.asarray(0, jnp.int32)
        stat_max = lax.dynamic_update_slice(stat_max, row_max[:, :, 0].T, (zero_row, stat_col))
        stat_sum = lax.dynamic_update_slice(stat_sum, row_sum[:, :, 0].T, (zero_row, stat_col))
        stat_dot = lax.dynamic_update_slice(stat_dot, row_dot[:, :, 0].T, (zero_row, stat_col))
        return (
            query_grad,
            band_kgrad,
            band_vgrad,
            mem_kgrad,
            mem_vgrad,
            attn_rows,
            stat_max,
            stat_sum,
            stat_dot,
        )

    init = (
        jnp.zeros((tokens, width), jnp.float32),
        jnp.zeros((W + tokens, width), jnp.float32),
        jnp.zeros((W + tokens, width), jnp.float32),
        jnp.zeros((slot_total, width), jnp.float32),
        jnp.zeros((slot_total, width), jnp.float32),
        jnp.zeros((tokens, width), jnp.bfloat16),
        jnp.zeros((W, heads_total), jnp.float32),
        jnp.zeros((W, heads_total), jnp.float32),
        jnp.zeros((W, heads_total), jnp.float32),
    )
    (
        query_grad,
        band_kgrad,
        band_vgrad,
        mem_kgrad,
        mem_vgrad,
        attn_rows,
        stat_max,
        stat_sum,
        stat_dot,
    ) = lax.fori_loop(0, pair_count, pair_step, init)
    own_kgrad = band_kgrad[W:]
    own_vgrad = band_vgrad[W:]
    back_kgrad, back_vgrad = (
        passed_along(band_kgrad[:W].astype(jnp.bfloat16), "ctx", -1).astype(jnp.float32),
        passed_along(band_vgrad[:W].astype(jnp.bfloat16), "ctx", -1).astype(jnp.float32),
    )
    own_kgrad = own_kgrad.at[tokens - W :].add(back_kgrad)
    own_vgrad = own_vgrad.at[tokens - W :].add(back_vgrad)
    got_kgrad, got_vgrad = (
        lax.psum_scatter(
            mem_kgrad.astype(jnp.bfloat16), "ctx", scatter_dimension=0, tiled=True
        ).astype(jnp.float32),
        lax.psum_scatter(
            mem_vgrad.astype(jnp.bfloat16), "ctx", scatter_dimension=0, tiled=True
        ).astype(jnp.float32),
    )
    own_kgrad = own_kgrad.at[own_slots].add(got_kgrad)
    own_vgrad = own_vgrad.at[own_slots].add(got_vgrad)
    weight_part = lax.dot_general(
        attn_rows, grad_out, (((0,), (0,)), ((), ())), preferred_element_type=jnp.float32
    )
    weight_total = lax.psum(weight_part, ("fam", "ctx"))
    weight_grad = weight_total * (lax.axis_size("fam") * ctx_size * tokens) ** (-0.5)
    return (
        query_grad.astype(jnp.bfloat16)[None],
        own_kgrad.astype(jnp.bfloat16)[None],
        own_vgrad.astype(jnp.bfloat16)[None],
        weight_grad,
    )


def solution(mesh):
    return jax.shard_map(
        per_device,
        mesh=mesh,
        in_specs=(
            P("fam", "ctx", None),
            P("fam", "ctx", None),
            P("fam", "ctx", None),
            P("fam", "ctx", None),
            P(),
            P("fam", None),
            P("fam", None),
            P("fam", None),
        ),
        out_specs=(P("fam", "ctx", None), P("fam", "ctx", None), P("fam", "ctx", None), P()),
        check_vma=False,
    )
```

profile of v0, /device:TPU:1, one launch (start us, length us, event | category | flops | bytes accessed | tf_op | source)
XLA Modules:
  0.0 967.8 jit_solution(17995845950725439622)
XLA Ops:
  33.3 6.4 collective-permute-done
  44.0 19.9 %all-gather.7.cloned.1.call-done = bf16[512,1024]{1,0:T(8,128)(2,1)} async-done(((bf16[16,1024]{1,0:T(8,128)(2,1)}), bf16[512,1024]{1,0:T(8,128)(2,1)}) %all-gather.7.cloned.1.call-update) | async-done | bytes 1048592 | tf_op jit(solution)/shard_map/all_gather | solution.py:110
  63.9 44.9 %all-gather.5.cloned.1.call-done = bf16[512,1024]{1,0:T(8,128)(2,1)} async-done(((bf16[16,1024]{1,0:T(8,128)(2,1)}), bf16[512,1024]{1,0:T(8,128)(2,1)}) %all-gather.5.cloned.1.call-update) | async-done | bytes 1048592 | tf_op jit(solution)/shard_map/all_gather | solution.py:109
  118.0 518.4 %while.27 = (s32[]{:T(128)}, bf16[512,1024]{1,0:T(8,128)(2,1)}, f32[1024,1024]{1,0:T(8,128)}, f32[1024,1024]{1,0:T(8,128)}, f32[512,1024]{1,0:T(8,128)}, /*index...) while((s32[]{:T(128)}, bf16[512,1024]{1,0:T(8,128)(2,1)}, ...), condition=%wide.region_14.15_spmd, body=%wide.region_10.14_spmd.sunk | while | flops 1247747584 | bytes 80244984 | solution.py:202
  132.8 7.0 fusion.100
  144.4 13.6 %fusion.101 = bf16[2,64,512]{2,1,0:T(8,128)(2,1)S(1)} fusion(f32[2,512,1536]{2,1,0:T(8,128)} %fusion.99, bf16[512,2,64]{0,2,1:T(8,128)(2,1)S(1)} %bitcast.109, bf16[1024,2,64]{0,2,1:T(8,128)(2,1)S(1)} %bitcast.104, f32[2,512,1536]{2,1,0:T(8,128)} %get-tuple-element.467, f32[2,512]{1,0:T(2,128)S(1)} %broadcast_maximum_fusion.2), kind=kOutput, calls=%fused_computation.16.clone.1 | convolution fusion | flops 213125632 | bytes 13111296 | tf_op jit(solution)/shard_map/while/body/eval_jaxpr/gqk,kge->qge/dot_general | solution.py:77
  157.9 13.2 %fusion.102 = f32[1536,2,64]{0,2,1:T(8,128)S(1)} fusion(bf16[512,2,64]{0,2,1:T(8,128)(2,1)S(1)} %bitcast.107, f32[2,512,1536]{2,1,0:T(8,128)} %fusion.99, f32[2,512,1536]{2,1,0:T(8,128)} %get-tuple-element.467, f32[2,512]{1,0:T(2,128)S(1)} %broadcast_maximum_fusion.2), kind=kOutput, calls=%fused_computation.18.clone.1 | convolution fusion | flops 212339200 | bytes 13504512 | tf_op jit(solution)/shard_map/while/body/eval_jaxpr/gqk,qge->kge/dot_general | solution.py:78
  197.6 7.0 fusion.100
  209.2 13.6 %fusion.101 = bf16[2,64,512]{2,1,0:T(8,128)(2,1)S(1)} fusion(f32[2,512,1536]{2,1,0:T(8,128)} %fusion.99, bf16[512,2,64]{0,2,1:T(8,128)(2,1)S(1)} %bitcast.109, bf16[1024,2,64]{0,2,1:T(8,128)(2,1)S(1)} %bitcast.104, f32[2,512,1536]{2,1,0:T(8,128)} %get-tuple-element.467, f32[2,512]{1,0:T(2,128)S(1)} %broadcast_maximum_fusion.2), kind=kOutput, calls=%fused_computation.16.clone.1 | convolution fusion | flops 213125632 | bytes 13111296 | tf_op jit(solution)/shard_map/while/body/eval_jaxpr/gqk,kge->qge/dot_general | solution.py:77
  222.7 13.2 %fusion.102 = f32[1536,2,64]{0,2,1:T(8,128)S(1)} fusion(bf16[512,2,64]{0,2,1:T(8,128)(2,1)S(1)} %bitcast.107, f32[2,512,1536]{2,1,0:T(8,128)} %fusion.99, f32[2,512,1536]{2,1,0:T(8,128)} %get-tuple-element.467, f32[2,512]{1,0:T(2,128)S(1)} %broadcast_maximum_fusion.2), kind=kOutput, calls=%fused_computation.18.clone.1 | convolution fusion | flops 212339200 | bytes 13504512 | tf_op jit(solution)/shard_map/while/body/eval_jaxpr/gqk,qge->kge/dot_general | solution.py:78
  262.4 7.0 fusion.100
  274.0 13.6 %fusion.101 = bf16[2,64,512]{2,1,0:T(8,128)(2,1)S(1)} fusion(f32[2,512,1536]{2,1,0:T(8,128)} %fusion.99, bf16[512,2,64]{0,2,1:T(8,128)(2,1)S(1)} %bitcast.109, bf16[1024,2,64]{0,2,1:T(8,128)(2,1)S(1)} %bitcast.104, f32[2,512,1536]{2,1,0:T(8,128)} %get-tuple-element.467, f32[2,512]{1,0:T(2,128)S(1)} %broadcast_maximum_fusion.2), kind=kOutput, calls=%fused_computation.16.clone.1 | convolution fusion | flops 213125632 | bytes 13111296 | tf_op jit(solution)/shard_map/while/body/eval_jaxpr/gqk,kge->qge/dot_general | solution.py:77
  287.5 13.2 %fusion.102 = f32[1536,2,64]{0,2,1:T(8,128)S(1)} fusion(bf16[512,2,64]{0,2,1:T(8,128)(2,1)S(1)} %bitcast.107, f32[2,512,1536]{2,1,0:T(8,128)} %fusion.99, f32[2,512,1536]{2,1,0:T(8,128)} %get-tuple-element.467, f32[2,512]{1,0:T(2,128)S(1)} %broadcast_maximum_fusion.2), kind=kOutput, calls=%fused_computation.18.clone.1 | convolution fusion | flops 212339200 | bytes 13504512 | tf_op jit(solution)/shard_map/while/body/eval_jaxpr/gqk,qge->kge/dot_general | solution.py:78
  327.2 7.0 fusion.100
  338.8 13.6 %fusion.101 = bf16[2,64,512]{2,1,0:T(8,128)(2,1)S(1)} fusion(f32[2,512,1536]{2,1,0:T(8,128)} %fusion.99, bf16[512,2,64]{0,2,1:T(8,128)(2,1)S(1)} %bitcast.109, bf16[1024,2,64]{0,2,1:T(8,128)(2,1)S(1)} %bitcast.104, f32[2,512,1536]{2,1,0:T(8,128)} %get-tuple-element.467, f32[2,512]{1,0:T(2,128)S(1)} %broadcast_maximum_fusion.2), kind=kOutput, calls=%fused_computation.16.clone.1 | convolution fusion | flops 213125632 | bytes 13111296 | tf_op jit(solution)/shard_map/while/body/eval_jaxpr/gqk,kge->qge/dot_general | solution.py:77
  352.4 13.2 %fusion.102 = f32[1536,2,64]{0,2,1:T(8,128)S(1)} fusion(bf16[512,2,64]{0,2,1:T(8,128)(2,1)S(1)} %bitcast.107, f32[2,512,1536]{2,1,0:T(8,128)} %fusion.99, f32[2,512,1536]{2,1,0:T(8,128)} %get-tuple-element.467, f32[2,512]{1,0:T(2,128)S(1)} %broadcast_maximum_fusion.2), kind=kOutput, calls=%fused_computation.18.clone.1 | convolution fusion | flops 212339200 | bytes 13504512 | tf_op jit(solution)/shard_map/while/body/eval_jaxpr/gqk,qge->kge/dot_general | solution.py:78
  392.0 7.0 fusion.100
  403.6 13.6 %fusion.101 = bf16[2,64,512]{2,1,0:T(8,128)(2,1)S(1)} fusion(f32[2,512,1536]{2,1,0:T(8,128)} %fusion.99, bf16[512,2,64]{0,2,1:T(8,128)(2,1)S(1)} %bitcast.109, bf16[1024,2,64]{0,2,1:T(8,128)(2,1)S(1)} %bitcast.104, f32[2,512,1536]{2,1,0:T(8,128)} %get-tuple-element.467, f32[2,512]{1,0:T(2,128)S(1)} %broadcast_maximum_fusion.2), kind=kOutput, calls=%fused_computation.16.clone.1 | convolution fusion | flops 213125632 | bytes 13111296 | tf_op jit(solution)/shard_map/while/body/eval_jaxpr/gqk,kge->qge/dot_general | solution.py:77
  417.2 13.2 %fusion.102 = f32[1536,2,64]{0,2,1:T(8,128)S(1)} fusion(bf16[512,2,64]{0,2,1:T(8,128)(2,1)S(1)} %bitcast.107, f32[2,512,1536]{2,1,0:T(8,128)} %fusion.99, f32[2,512,1536]{2,1,0:T(8,128)} %get-tuple-element.467, f32[2,512]{1,0:T(2,128)S(1)} %broadcast_maximum_fusion.2), kind=kOutput, calls=%fused_computation.18.clone.1 | convolution fusion | flops 212339200 | bytes 13504512 | tf_op jit(solution)/shard_map/while/body/eval_jaxpr/gqk,qge->kge/dot_general | solution.py:78
  456.9 7.0 fusion.100
  468.4 13.6 %fusion.101 = bf16[2,64,512]{2,1,0:T(8,128)(2,1)S(1)} fusion(f32[2,512,1536]{2,1,0:T(8,128)} %fusion.99, bf16[512,2,64]{0,2,1:T(8,128)(2,1)S(1)} %bitcast.109, bf16[1024,2,64]{0,2,1:T(8,128)(2,1)S(1)} %bitcast.104, f32[2,512,1536]{2,1,0:T(8,128)} %get-tuple-element.467, f32[2,512]{1,0:T(2,128)S(1)} %broadcast_maximum_fusion.2), kind=kOutput, calls=%fused_computation.16.clone.1 | convolution fusion | flops 213125632 | bytes 13111296 | tf_op jit(solution)/shard_map/while/body/eval_jaxpr/gqk,kge->qge/dot_general | solution.py:77
  482.0 13.2 %fusion.102 = f32[1536,2,64]{0,2,1:T(8,128)S(1)} fusion(bf16[512,2,64]{0,2,1:T(8,128)(2,1)S(1)} %bitcast.107, f32[2,512,1536]{2,1,0:T(8,128)} %fusion.99, f32[2,512,1536]{2,1,0:T(8,128)} %get-tuple-element.467, f32[2,512]{1,0:T(2,128)S(1)} %broadcast_maximum_fusion.2), kind=kOutput, calls=%fused_computation.18.clone.1 | convolution fusion | flops 212339200 | bytes 13504512 | tf_op jit(solution)/shard_map/while/body/eval_jaxpr/gqk,qge->kge/dot_general | solution.py:78
  521.6 7.0 fusion.100
  533.2 13.6 %fusion.101 = bf16[2,64,512]{2,1,0:T(8,128)(2,1)S(1)} fusion(f32[2,512,1536]{2,1,0:T(8,128)} %fusion.99, bf16[512,2,64]{0,2,1:T(8,128)(2,1)S(1)} %bitcast.109, bf16[1024,2,64]{0,2,1:T(8,128)(2,1)S(1)} %bitcast.104, f32[2,512,1536]{2,1,0:T(8,128)} %get-tuple-element.467, f32[2,512]{1,0:T(2,128)S(1)} %broadcast_maximum_fusion.2), kind=kOutput, calls=%fused_computation.16.clone.1 | convolution fusion | flops 213125632 | bytes 13111296 | tf_op jit(solution)/shard_map/while/body/eval_jaxpr/gqk,kge->qge/dot_general | solution.py:77
  546.8 13.2 %fusion.102 = f32[1536,2,64]{0,2,1:T(8,128)S(1)} fusion(bf16[512,2,64]{0,2,1:T(8,128)(2,1)S(1)} %bitcast.107, f32[2,512,1536]{2,1,0:T(8,128)} %fusion.99, f32[2,512,1536]{2,1,0:T(8,128)} %get-tuple-element.467, f32[2,512]{1,0:T(2,128)S(1)} %broadcast_maximum_fusion.2), kind=kOutput, calls=%fused_computation.18.clone.1 | convolution fusion | flops 212339200 | bytes 13504512 | tf_op jit(solution)/shard_map/while/body/eval_jaxpr/gqk,qge->kge/dot_general | solution.py:78
  586.4 7.0 fusion.100
  598.0 13.6 %fusion.101 = bf16[2,64,512]{2,1,0:T(8,128)(2,1)S(1)} fusion(f32[2,512,1536]{2,1,0:T(8,128)} %fusion.99, bf16[512,2,64]{0,2,1:T(8,128)(2,1)S(1)} %bitcast.109, bf16[1024,2,64]{0,2,1:T(8,128)(2,1)S(1)} %bitcast.104, f32[2,512,1536]{2,1,0:T(8,128)} %get-tuple-element.467, f32[2,512]{1,0:T(2,128)S(1)} %broadcast_maximum_fusion.2), kind=kOutput, calls=%fused_computation.16.clone.1 | convolution fusion | flops 213125632 | bytes 13111296 | tf_op jit(solution)/shard_map/while/body/eval_jaxpr/gqk,kge->qge/dot_general | solution.py:77
  611.6 13.2 %fusion.102 = f32[1536,2,64]{0,2,1:T(8,128)S(1)} fusion(bf16[512,2,64]{0,2,1:T(8,128)(2,1)S(1)} %bitcast.107, f32[2,512,1536]{2,1,0:T(8,128)} %fusion.99, f32[2,512,1536]{2,1,0:T(8,128)} %get-tuple-element.467, f32[2,512]{1,0:T(2,128)S(1)} %broadcast_maximum_fusion.2), kind=kOutput, calls=%fused_computation.18.clone.1 | convolution fusion | flops 212339200 | bytes 13504512 | tf_op jit(solution)/shard_map/while/body/eval_jaxpr/gqk,qge->kge/dot_general | solution.py:78
  660.6 9.2 collective-permute-done.2
  671.4 43.8 %reduce-scatter.5.cloned.1.call-done = bf16[16,1024]{1,0:T(8,128)(2,1)} async-done(((bf16[512,1024]{1,0:T(8,128)(2,1)}), bf16[16,1024]{1,0:T(8,128)(2,1)}) %reduce-scatter.5.cloned.1.call-update) | async-done | bytes 32784 | tf_op jit(solution)/shard_map/reduce_scatter | solution.py:215
  716.9 79.4 %reduce-scatter.3.cloned.1.call-done = bf16[16,1024]{1,0:T(8,128)(2,1)} async-done(((bf16[512,1024]{1,0:T(8,128)(2,1)}), bf16[16,1024]{1,0:T(8,128)(2,1)}) %reduce-scatter.3.cloned.1.call-update) | async-done | bytes 32784 | tf_op jit(solution)/shard_map/reduce_scatter | solution.py:212
  804.2 152.1 %all-reduce.2.cloned.1.call-done = f32[1024,1024]{1,0:T(8,128)} async-done(((f32[1024,1024]{1,0:T(8,128)}), f32[1024,1024]{1,0:T(8,128)}) %all-reduce.2.cloned.1.call-update) | async-done | bytes 4194320 | tf_op jit(solution)/shard_map/psum | solution.py:224
  (395 shorter events, 327.0 us)
Async XLA Ops:
  7.2 22.5 %copy-start = (bf16[1024,1024]{1,0:T(8,128)(2,1)S(1)}, bf16[1024,1024]{1,0:T(8,128)(2,1)}, u32[]{:S(2)}) copy-start(bf16[1024,1024]{1,0:T(8,128)(2,1)} %param.22) | copy-start | bytes 6291460
  7.2 56.7 %all-gather.7.cloned.1.call-start = ((), (), s32[]{:S(2)}) async-start(), calls=%async_computation.6 | async-start | bytes 1081344 | tf_op jit(solution)/shard_map/all_gather | solution.py:110
  8.1 0.5 copy-start.6
  11.2 97.5 %all-gather.5.cloned.1.call-start = ((), (), s32[]{:S(2)}) async-start(), calls=%async_computation.5 | async-start | bytes 1081344 | tf_op jit(solution)/shard_map/all_gather | solution.py:109
  11.3 31.3 %collective-permute-start.1 = (bf16[512,1024]{1,0:T(8,128)(2,1)}, bf16[512,1024]{1,0:T(8,128)(2,1)S(1)}, u32[]{:S(2)}, u32[]{:S(2)}) collective-permute-start(bf16[512,1024]{1,0:T(8,128)(2,1)} %bitcast.115), channel_id=1, source_target_pairs={{0,1},{1,2},{2,3},{3,4},{4,5},{5,6},{6,7},{7,8},{8,9},{9,10},{10,1... | collective-permute-start | bytes 3145736 | tf_op jit(solution)/shard_map/ppermute | solution.py:17
  15.9 23.8 %collective-permute-start = (bf16[512,1024]{1,0:T(8,128)(2,1)}, bf16[512,1024]{1,0:T(8,128)(2,1)}, u32[]{:S(2)}, u32[]{:S(2)}) collective-permute-start(bf16[512,1024]{1,0:T(8,128)(2,1)} %bitcast.111), channel_id=1, source_target_pairs={{0,1},{1,2},{2,3},{3,4},{4,5},{5,6},{6,7},{7,8},{8,9},{9,10},{10,1... | collective-permute-start | bytes 3145736 | tf_op jit(solution)/shard_map/ppermute | solution.py:17
  20.4 694.8 %reduce-scatter.5.cloned.1.call-start = ((), (), s32[]{:S(2)}) async-start(), calls=%async_computation.3 | async-start | bytes 1081344 | tf_op jit(solution)/shard_map/reduce_scatter | solution.py:215
  29.7 10.0 %copy-start.4 = (bf16[1,512,1024]{2,1,0:T(8,128)(2,1)S(1)}, bf16[1,512,1024]{2,1,0:T(8,128)(2,1)}, u32[]{:S(2)}) copy-start(bf16[1,512,1024]{2,1,0:T(8,128)(2,1)} %param.19) | copy-start | bytes 3145732
  33.3 9.3 copy-start.5
  636.4 3.1 copy-start.3
  639.4 156.9 %reduce-scatter.3.cloned.1.call-start = ((), (), s32[]{:S(2)}) async-start(), calls=%async_computation.2 | async-start | bytes 1081344 | tf_op jit(solution)/shard_map/reduce_scatter | solution.py:212
  640.7 315.6 %all-reduce.2.cloned.1.call-start = ((), (), s32[]{:S(2)}) async-start(), calls=%async_computation.4 | async-start | bytes 8388608 | tf_op jit(solution)/shard_map/psum | solution.py:224
  642.5 16.1 %collective-permute-start.3 = (bf16[512,1024]{1,0:T(8,128)(2,1)S(1)}, bf16[512,1024]{1,0:T(8,128)(2,1)S(1)}, u32[]{:S(2)}, u32[]{:S(2)}) collective-permute-start(bf16[512,1024]{1,0:T(8,128)(2,1)S(1)} %slice.88), channel_id=1, source_target_pairs={{1,0},{2,1},{3,2},{4,3},{5,4},{6,5},{7,6},{8,7},{9,8},{10,9},{11,1... | collective-permute-start | bytes 3145736 | tf_op jit(solution)/shard_map/ppermute | solution.py:17
  649.6 20.2 %copy-start.2 = (f32[1024,1024]{1,0:T(8,128)S(1)}, f32[1024,1024]{1,0:T(8,128)}, u32[]{:S(2)}) copy-start(f32[1024,1024]{1,0:T(8,128)} %get-tuple-element.279) | copy-start | bytes 12582916
  651.6 18.3 %collective-permute-start.2 = (bf16[512,1024]{1,0:T(8,128)(2,1)S(1)}, bf16[512,1024]{1,0:T(8,128)(2,1)S(1)}, u32[]{:S(2)}, u32[]{:S(2)}) collective-permute-start(bf16[512,1024]{1,0:T(8,128)(2,1)S(1)} %slice.89), channel_id=1, source_target_pairs={{1,0},{2,1},{3,2},{4,3},{5,4},{6,5},{7,6},{8,7},{9,8},{10,9},{11,1... | collective-permute-start | bytes 3145736 | tf_op jit(solution)/shard_map/ppermute | solution.py:17
  801.3 160.0 %copy-start.1 = (bf16[1024,1024]{1,0:T(8,128)(2,1)S(1)}, bf16[1024,1024]{1,0:T(8,128)(2,1)}, u32[]{:S(2)}) copy-start(bf16[1024,1024]{1,0:T(8,128)(2,1)} %param.22) | copy-start | bytes 6291460
Sparse Core Ops, SparseCore 0:
  11.4 52.4 all-gather.6
  66.7 41.9 all-gather.4
  639.6 75.6 reduce-scatter.4
  719.5 76.7 reduce-scatter.2
  801.1 155.0 all-reduce.1
where the time goes:
time: 972 us; the launch traced here: 968 us
  matrix products  379 us (39%)
  waiting for transfers between devices  361 us (37%)
  local copies, waits for them, and re-layouts  166 us (17%)
  other arithmetic  35.4 us (4%)
  between operations  13.9 us (1%)
  starting transfers between devices  11.1 us (1%)
    psum x1, waiting for transfers between devices, per_device(): weight_total = lax.psum(weight_part, ('fam', 'ctx'))  152 us
    dot_general x8, matrix products, attend(): jnp.einsum('gqk,kge->qge', grad_score, key_blk, preferred_element_type=jn...  108 us
    dot_general x8, matrix products, attend(): jnp.einsum('gqk,qge->kge', grad_score, query_blk, preferred_element_type=...  105 us
    reduce_scatter x1, waiting for transfers between devices, per_device(): lax.psum_scatter(mem_kgrad.astype(jnp.bfloat16), 'ctx', scatter_dimension...  79.4 us
    sub x8, matrix products, attend(): expo = jnp.where(live, jnp.exp(shifted - row_max), 0.0)  56 us
    dynamic_slice x88, local copies, waits for them, and re-layouts, columns_of(): return lax.dynamic_slice_in_dim(array, column, span, 1)  50 us
    all_gather x1, waiting for transfers between devices, per_device(): lax.all_gather(key_loc[own_slots], 'ctx', axis=0, tiled=True)  44.9 us
    reduce_scatter x1, waiting for transfers between devices, per_device(): lax.psum_scatter(mem_vgrad.astype(jnp.bfloat16), 'ctx', scatter_dimension...  43.8 us
  transfers between devices with their start and end apart: 9, of which 8 were waited for; matrix products, arithmetic and copies ran while one was open for 4% of the time, Pallas kernels for 0%

commit v1 on v0

v1 whole, which is shorter than its diff:
```python
import functools
import jax, jax.numpy as jnp
from jax import lax
from jax.sharding import PartitionSpec as P
from jax.experimental import pallas as pl
from jax.experimental.pallas import tpu as pltpu
F32=jnp.float32; BF=jnp.bfloat16
NEG=-1e30
def nt(a,b): return lax.dot_general(a,b,(((1,),(1,)),((),())),preferred_element_type=F32)
def nn(a,b): return lax.dot_general(a,b,(((1,),(0,)),((),())),preferred_element_type=F32)
def tn(a,b): return lax.dot_general(a,b,(((0,),(0,)),((),())),preferred_element_type=F32)
def make(QB, VM=60):
  NB=512//QB; KB=512+QB
  def kernel(q_ref,k_ref,v_ref,hk_ref,hv_ref,mk_ref,mv_ref,cot_ref,w_ref,kb_ref,valid_ref,
             dq_ref,dk_ref,dv_ref,w_out, kx,vx,dkt,dvt,att_ref):
    p=pl.program_id(0)
    @pl.when(p==0)
    def _():
      kx[:,128:]=kb_ref[...]
      l2=lax.broadcasted_iota(jnp.int32,(1536,128),1)
      vx[:,128:]=jnp.where(l2<2,1.0,0.0).astype(BF)
    kx[0:512,:128]=hk_ref[...]; kx[512:1024,:128]=k_ref[...]; kx[1024:1536,:128]=mk_ref[...]
    vx[0:512,:128]=hv_ref[...]; vx[512:1024,:128]=v_ref[...]; vx[1024:1536,:128]=mv_ref[...]
    do=nt(cot_ref[...],w_ref[...]).astype(BF)
    dkt[...]=jnp.zeros_like(dkt); dvt[...]=jnp.zeros_like(dvt)
    lane=lax.broadcasted_iota(jnp.int32,(QB,128),1); lo=lane<64
    lane2=lax.broadcasted_iota(jnp.int32,(2*QB,128),1)
    row2=lax.broadcasted_iota(jnp.int32,(2*QB,128),0)
    rr=lax.broadcasted_iota(jnp.int32,(2*QB,QB),0); rr=jnp.where(rr>=QB,rr-QB,rr)
    cc=lax.broadcasted_iota(jnp.int32,(2*QB,QB),1)
    tri_far=cc>rr; tri_near=cc<=rr
    z=jnp.zeros((QB,128),BF)
    for b in range(NB):
      rows=slice(b*QB,(b+1)*QB); band=slice(b*QB,b*QB+KB); mem=slice(1024,1536)
      qp=q_ref[rows,:]*jnp.asarray(0.125,BF)
      qs=jnp.concatenate([jnp.where(lo,qp,z),jnp.where(lo,z,qp)],0)
      r2=jnp.where(row2>=QB,row2-QB,row2)+b*QB
      oh=jnp.where(lane2==r2//128,1.0,0.0).astype(BF)
      qa=jnp.concatenate([qs,oh],1)
      sb=nt(qa,kx[band,:]); sm=nt(qa,kx[mem,:])
      s0=jnp.where(tri_far,sb[:,:QB],NEG); s2=jnp.where(tri_near,sb[:,512:],NEG)
      if QB<512: parts=[s0,sb[:,QB:512],s2,sm]
      else: parts=[s0,s2,sm]
      s=jnp.concatenate(parts,1)
      m=jnp.max(s,axis=1,keepdims=True)
      e=jnp.exp(s-m).astype(BF)
      eb=e[:,:KB]; em=e[:,KB:]
      o=nn(eb,vx[band,:])+nn(em,vx[mem,:])
      vl=valid_ref[rows,:]; vl=jnp.concatenate([vl,vl],0)
      inv=vl/jnp.maximum(o[:,128:129],1.0)
      att=o[:,:128]*inv
      dop=do[rows,:]
      dos=jnp.concatenate([jnp.where(lo,dop,z),jnp.where(lo,z,dop)],0)
      dosf=dos.astype(F32)
      rd=jnp.sum(att*dosf,axis=1,keepdims=True)
      hi=rd.astype(BF).astype(F32)
      pat=jnp.where(lane2==0,-hi,jnp.where(lane2==1,hi-rd,0.0)).astype(BF)
      da=jnp.concatenate([dos,pat],1)
      dpb=nt(da,vx[band,:]); dpm=nt(da,vx[mem,:])
      dsb=(eb.astype(F32)*dpb).astype(BF); dsm=(em.astype(F32)*dpm).astype(BF)
      dqs=nn(dsb,kx[band,:128])+nn(dsm,kx[mem,:128])
      dqs=dqs*(inv*0.125)
      dq_ref[rows,:]=jnp.where(lo,dqs[:QB],dqs[QB:]).astype(BF)
      att_ref[rows,:]=jnp.where(lo,att[:QB],att[QB:]).astype(BF)
      qn=(qs.astype(F32)*inv).astype(BF); don=(dosf*inv).astype(BF)
      dkt[:,band]+=tn(qn,dsb); dkt[:,mem]+=tn(qn,dsm)
      dvt[:,band]+=tn(don,eb); dvt[:,mem]+=tn(don,em)
    dk_ref[...]=dkt[...].T
    dv_ref[...]=dvt[...].T
    w_out[...]=tn(att_ref[...],cot_ref[...])
  def call(q,k,v,hk,hv,mk,mv,cot,w,kb,valid):
    col=pl.BlockSpec((512,128),lambda p:(0,p))
    full=lambda s: pl.BlockSpec(s,lambda p:(0,0))
    return pl.pallas_call(kernel,grid=(8,),
      in_specs=[col]*7+[full((512,1024)),pl.BlockSpec((128,1024),lambda p:(p,0)),full((1536,128)),full((512,1))],
      out_specs=[col,pl.BlockSpec((1536,128),lambda p:(0,p)),pl.BlockSpec((1536,128),lambda p:(0,p)),pl.BlockSpec((128,1024),lambda p:(p,0))],
      out_shape=[jax.ShapeDtypeStruct((512,1024),BF),jax.ShapeDtypeStruct((1536,1024),F32),jax.ShapeDtypeStruct((1536,1024),F32),jax.ShapeDtypeStruct((1024,1024),F32)],
      scratch_shapes=[pltpu.VMEM((1536,256),BF),pltpu.VMEM((1536,256),BF),pltpu.VMEM((128,1536),F32),pltpu.VMEM((128,1536),F32),pltpu.VMEM((512,128),BF)],
      compiler_params=pltpu.CompilerParams(vmem_limit_bytes=VM*2**20),name='attn')(q,k,v,hk,hv,mk,mv,cot,w,kb,valid)
  return call


def protein_tables(prot_blocks, last_fill):
    count = prot_blocks.shape[0]
    index = jnp.arange(count, dtype=jnp.int32)
    ends = jnp.sum(jnp.where(index[None, :] <= index[:, None], prot_blocks[None, :], 0), axis=1)
    return ends, ends - prot_blocks, (prot_blocks - 1) * 128 + last_fill


def token_info(positions, tables):
    ends, starts, filled = tables
    block = jnp.floor_divide(positions, 128)
    protein = jnp.sum((block[:, None] >= ends[None, :]).astype(jnp.int32), axis=1)
    hit = protein[:, None] == jnp.arange(ends.shape[0], dtype=jnp.int32)[None, :]
    first = jnp.sum(jnp.where(hit, starts[None, :], 0), axis=1)
    limit = jnp.sum(jnp.where(hit, filled[None, :], 0), axis=1)
    return protein, (positions >= 0) & (positions - first * 128 < limit)


def per_device(queries, key_rows, value_rows, cotangent, out_weight, prot_blocks, last_fill, memory_slots):
    q, k, v, cot = queries[0], key_rows[0], value_rows[0], cotangent[0]
    tables = protein_tables(prot_blocks[0], last_fill[0])
    slots = memory_slots[0]
    me = lax.axis_index("ctx")
    base = me * 512
    ext = base - 512 + jnp.arange(1024, dtype=jnp.int32)
    source = jnp.arange(512, dtype=jnp.int32) // 16 * 512 + slots
    ext_prot, ext_ok = token_info(ext, tables)
    mem_prot, mem_ok = token_info(source, tables)
    block_prot = ext_prot[512::128]
    band = ext_ok[:, None] & (ext_prot[:, None] == block_prot[None, :])
    memory = mem_ok[:, None] & (mem_prot[:, None] < block_prot[None, :])
    seen = jnp.concatenate([band, memory], 0)
    bias = jnp.pad(jnp.where(seen, 0.0, NEG).astype(BF), ((0, 0), (0, 124)))
    valid = ext_ok[512:].astype(F32)[:, None]
    own = lax.dynamic_slice_in_dim(slots, me * 16, 16)
    pick = (own[:, None] == jnp.arange(512, dtype=jnp.int32)[None, :]).astype(BF)
    mk = lax.all_gather(nn(pick, k).astype(BF), "ctx", axis=0, tiled=True)
    mv = lax.all_gather(nn(pick, v).astype(BF), "ctx", axis=0, tiled=True)
    ahead = [(i, i + 1) for i in range(31)]
    back = [(i + 1, i) for i in range(31)]
    hk, hv = lax.ppermute((k, v), "ctx", ahead)
    dq, dk, dv, weight = make(256)(q, k, v, hk, hv, mk, mv, cot, out_weight, bias, valid)
    weight = lax.psum(weight, ("fam", "ctx")) * (4 * 16384) ** -0.5
    bk, bv = lax.ppermute((dk[:512].astype(BF), dv[:512].astype(BF)), "ctx", back)
    gk = lax.psum_scatter(dk[1024:].astype(BF), "ctx", scatter_dimension=0, tiled=True)
    gv = lax.psum_scatter(dv[1024:].astype(BF), "ctx", scatter_dimension=0, tiled=True)
    dk = dk[512:1024] + bk.astype(F32) + tn(pick, gk)
    dv = dv[512:1024] + bv.astype(F32) + tn(pick, gv)
    return dq[None], dk.astype(BF)[None], dv.astype(BF)[None], weight


def solution(mesh):
    row = P("fam", "ctx", None)
    fam = P("fam", None)
    return jax.shard_map(
        per_device,
        mesh=mesh,
        in_specs=(row, row, row, row, P(), fam, fam, fam),
        out_specs=(row, row, row, P()),
        check_vma=False,
    )
```

time: 972 us -> 499 us (0.51)
  matrix products: 379 us -> 10.5 us
  local copies, waits for them, and re-layouts: 166 us -> 5.46 us
  Pallas kernels: 0 us -> 57.5 us
  waiting for transfers between devices: 361 us -> 385 us
  other arithmetic: 35.4 us -> 15 us
    dot_general x42 -> x4, matrix products: 323 us -> 10.5 us  [the longest x2 6.27 us: tn(): lax.dot_general(a, b, (((0,), (0,)), ((), ())), preferred_element_type=F32)]
    dynamic_slice x152 -> x0, local copies, waits for them, and re-layouts: 88.2 us -> none  [the longest x88 50 us: columns_of(): return lax.dynamic_slice_in_dim(array, column, span, 1)]
    pallas_call x0 -> x1, Pallas kernels: none -> 57.5 us  [call(): pl.pallas_call(kernel, grid=(8,), in_specs=[col] * 7 + [full((512, 1024))...]
    sub x8 -> x0, matrix products: 56 us -> none  [attend(): expo = jnp.where(live, jnp.exp(shifted - row_max), 0.0)]
    dynamic_update_slice x72 -> x0, local copies, waits for them, and re-layouts: 39.2 us -> none  [the longest x48 20.3 us: add_into(): lax.dynamic_update_slice(target, current + update, (row_index, column))]
    slice x34 -> x3, local copies, waits for them, and re-layouts: 20.5 us -> 2.75 us  [the longest x1 1.52 us: per_device(): dv[:512].astype(BF)]
where the time goes in v1:
time: 499 us; the launch traced here: 498 us
  waiting for transfers between devices  385 us (77%)
  Pallas kernels  57.5 us (12%)
  other arithmetic  15 us (3%)
  between operations  13.9 us (3%)
  starting transfers between devices  10.8 us (2%)
  matrix products  10.5 us (2%)
  local copies, waits for them, and re-layouts  5.46 us (1%)
    psum x1, waiting for transfers between devices, per_device(): weight = lax.psum(weight, ('fam', 'ctx')) * (4 * 16384) ** (-0.5)  157 us
    reduce_scatter x1, waiting for transfers between devices, per_device(): lax.psum_scatter(dv[1024:].astype(BF), 'ctx', scatter_dimension=0, tiled=...  77.4 us
    pallas_call x1, Pallas kernels, call(): pl.pallas_call(kernel, grid=(8,), in_specs=[col] * 7 + [full((512, 1024))...  57.5 us
    reduce_scatter x1, waiting for transfers between devices, per_device(): lax.psum_scatter(dk[1024:].astype(BF), 'ctx', scatter_dimension=0, tiled=...  54.4 us
    all_gather x1, waiting for transfers between devices, per_device(): mv = lax.all_gather(nn(pick, v).astype(BF), 'ctx', axis=0, tiled=True)  44.9 us
    all_gather x1, waiting for transfers between devices, per_device(): mk = lax.all_gather(nn(pick, k).astype(BF), 'ctx', axis=0, tiled=True)  24 us
    ppermute x2, waiting for transfers between devices, per_device(): hk, hv = lax.ppermute((k, v), 'ctx', ahead)  14.1 us
    ppermute x2, waiting for transfers between devices, per_device(): lax.ppermute((dk[:512].astype(BF), dv[:512].astype(BF)), 'ctx', back)  12 us
  transfers between devices with their start and end apart: 9, of which 8 were waited for; matrix products, arithmetic and copies ran while one was open for 4% of the time, Pallas kernels for 0%

profile of v1, /device:TPU:1, one launch (start us, length us, event | category | flops | bytes accessed | tf_op | source)
XLA Modules:
  0.0 498.0 jit_solution(16482886204293716246)
XLA Ops:
  7.2 0.7 dynamic-slice_bitcast_fusion
  7.9 2.1 convolution_convert_fusion.1
  10.1 4.6 collective-permute-start
  14.8 1.9 collective-permute-start.1
  16.7 2.1 convolution_convert_fusion
  18.9 0.8 select_reduce_fusion.4
  19.7 0.7 add_bitcast_fusion
  20.5 0.1 select_reduce_fusion.1
  20.6 0.7 add_select_fusion.1
  21.5 0.8 copy.22.valid_ref
  22.4 0.7 fusion.20
  23.3 0.3 copy.21
  23.5 0.9 pad.4.kb_ref
  24.4 2.6 collective-permute-done.hk_ref
  27.0 11.6 %collective-permute-done.1.hv_ref = bf16[512,1024]{1,0:T(8,128)(2,1)S(1)} collective-permute-done((bf16[512,1024]{1,0:T(8,128)(2,1)}, bf16[512,1024]{1,0:T(8,128)(2,1)S(1)}, u32[]{:S(2)}, u32[]{:S(2)}) %collective-permute-start.1) | collective-permute-done | bytes 1048608 | tf_op jit(solution)/shard_map/ppermute | solution.py:122
  38.6 24.0 %all-gather.3.cloned.1.call-done.mk_ref = bf16[512,1024]{1,0:T(8,128)(2,1)} async-done(((bf16[16,1024]{1,0:T(8,128)(2,1)}), bf16[512,1024]{1,0:T(8,128)(2,1)}) %all-gather.3.cloned.1.call-update) | async-done | bytes 1048592 | tf_op jit(solution)/shard_map/all_gather | solution.py:118
  62.6 44.9 %all-gather.5.cloned.1.call-done.mv_ref = bf16[512,1024]{1,0:T(8,128)(2,1)} async-done(((bf16[16,1024]{1,0:T(8,128)(2,1)}), bf16[512,1024]{1,0:T(8,128)(2,1)}) %all-gather.5.cloned.1.call-update) | async-done | bytes 1048592 | tf_op jit(solution)/shard_map/all_gather | solution.py:119
  107.5 57.5 %attn.1 = (bf16[512,1024]{1,0:T(8,128)(2,1)}, f32[1536,1024]{1,0:T(8,128)}, f32[1536,1024]{1,0:T(8,128)}, f32[1024,1024]{1,0:T(8,128)}) custom-call(bf16[512,1024]{1,0:T(8,128)(2,1)} %bitcast.32, bf16[512,1024]{1,0:T(8,128)(2,1)} %bitcast.29, bf16[512,1024]{1,0:T(8,128)(2,1)} %bitcast.31, bf16[512,1024]{1,0:T(8,128)(2,1)} %copy-done, ...), custom_call_target="tpu_custom_call" | custom-call | tf_op jit(solution)/shard_map/attn/pallas_call | solution.py:74
  164.9 3.3 convert.9
  168.2 1.1 fusion.25
  169.4 3.3 convert.10
  172.7 1.5 fusion.24
  174.3 0.5 all-reduce.3.cloned.1.call-update
  174.8 2.1 collective-permute-start.2
  177.0 1.9 collective-permute-start.3
  178.9 12.0 %collective-permute-done.2 = bf16[512,1024]{1,0:T(8,128)(2,1)S(1)} collective-permute-done((bf16[512,1024]{1,0:T(8,128)(2,1)S(1)}, bf16[512,1024]{1,0:T(8,128)(2,1)S(1)}, u32[]{:S(2)}, u32[]{:S(2)}) %collective-permute-start.2) | collective-permute-done | bytes 1048608 | tf_op jit(solution)/shard_map/ppermute | solution.py:125
  191.0 54.4 %reduce-scatter.3.cloned.1.call-done = bf16[16,1024]{1,0:T(8,128)(2,1)} async-done(((bf16[512,1024]{1,0:T(8,128)(2,1)}), bf16[16,1024]{1,0:T(8,128)(2,1)}) %reduce-scatter.3.cloned.1.call-update) | async-done | bytes 32784 | tf_op jit(solution)/shard_map/reduce_scatter | solution.py:126
  245.4 3.1 fusion
  248.5 77.4 %reduce-scatter.5.cloned.1.call-done = bf16[16,1024]{1,0:T(8,128)(2,1)} async-done(((bf16[512,1024]{1,0:T(8,128)(2,1)}), bf16[16,1024]{1,0:T(8,128)(2,1)}) %reduce-scatter.5.cloned.1.call-update) | async-done | bytes 32784 | tf_op jit(solution)/shard_map/reduce_scatter | solution.py:127
  325.9 3.1 fusion.1
  329.0 157.4 %all-reduce.3.cloned.1.call-done = f32[1024,1024]{1,0:T(8,128)} async-done(((f32[1024,1024]{1,0:T(8,128)}), f32[1024,1024]{1,0:T(8,128)}) %all-reduce.3.cloned.1.call-update) | async-done | bytes 4194320 | tf_op jit(solution)/shard_map/psum | solution.py:124
  486.4 5.0 %broadcast_multiply_fusion = f32[1024,1024]{1,0:T(8,128)} fusion(f32[1024,1024]{1,0:T(8,128)} %all-reduce.3.cloned.1.call-done), kind=kLoop, calls=%fused_computation | loop fusion | flops 1048576 | bytes 8388608 | tf_op jit(solution)/shard_map/mul | solution.py:124
  (24 shorter events, 0.8 us)
Async XLA Ops:
  7.2 55.4 %all-gather.3.cloned.1.call-start = ((), (), s32[]{:S(2)}) async-start(), calls=%async_computation.2 | async-start | bytes 1081344 | tf_op jit(solution)/shard_map/all_gather | solution.py:118
  10.1 97.4 %all-gather.5.cloned.1.call-start = ((), (), s32[]{:S(2)}) async-start(), calls=%async_computation.3 | async-start | bytes 1081344 | tf_op jit(solution)/shard_map/all_gather | solution.py:119
  10.1 16.8 %collective-permute-start = (bf16[512,1024]{1,0:T(8,128)(2,1)}, bf16[512,1024]{1,0:T(8,128)(2,1)S(1)}, u32[]{:S(2)}, u32[]{:S(2)}) collective-permute-start(bf16[512,1024]{1,0:T(8,128)(2,1)} %bitcast.28), channel_id=1, source_target_pairs={{0,1},{1,2},{2,3},{3,4},{4,5},{5,6},{6,7},{7,8},{8,9},{9,10},{10,1... | collective-permute-start | bytes 3145736 | tf_op jit(solution)/shard_map/ppermute | solution.py:122
  14.8 23.8 %collective-permute-start.1 = (bf16[512,1024]{1,0:T(8,128)(2,1)}, bf16[512,1024]{1,0:T(8,128)(2,1)S(1)}, u32[]{:S(2)}, u32[]{:S(2)}) collective-permute-start(bf16[512,1024]{1,0:T(8,128)(2,1)} %bitcast.30), channel_id=1, source_target_pairs={{0,1},{1,2},{2,3},{3,4},{4,5},{5,6},{6,7},{7,8},{8,9},{9,10},{10,1... | collective-permute-start | bytes 3145736 | tf_op jit(solution)/shard_map/ppermute | solution.py:122
  18.8 226.5 %reduce-scatter.3.cloned.1.call-start = ((), (), s32[]{:S(2)}) async-start(), calls=%async_computation.4 | async-start | bytes 1081344 | tf_op jit(solution)/shard_map/reduce_scatter | solution.py:126
  27.0 80.5 %copy-start = (bf16[512,1024]{1,0:T(8,128)(2,1)}, bf16[512,1024]{1,0:T(8,128)(2,1)S(1)}, u32[]{:S(2)}) copy-start(bf16[512,1024]{1,0:T(8,128)(2,1)S(1)} %collective-permute-done.hk_ref) | copy-start | bytes 3145732
  38.6 68.9 %copy-start.1 = (bf16[512,1024]{1,0:T(8,128)(2,1)}, bf16[512,1024]{1,0:T(8,128)(2,1)S(1)}, u32[]{:S(2)}) copy-start(bf16[512,1024]{1,0:T(8,128)(2,1)S(1)} %collective-permute-done.1.hv_ref) | copy-start | bytes 3145732
  169.4 156.5 %reduce-scatter.5.cloned.1.call-start = ((), (), s32[]{:S(2)}) async-start(), calls=%async_computation.5 | async-start | bytes 1081344 | tf_op jit(solution)/shard_map/reduce_scatter | solution.py:127
  174.2 312.2 %all-reduce.3.cloned.1.call-start = ((), (), s32[]{:S(2)}) async-start(), calls=%async_computation.6 | async-start | bytes 8388608 | tf_op jit(solution)/shard_map/psum | solution.py:124
  174.8 16.1 %collective-permute-start.2 = (bf16[512,1024]{1,0:T(8,128)(2,1)S(1)}, bf16[512,1024]{1,0:T(8,128)(2,1)S(1)}, u32[]{:S(2)}, u32[]{:S(2)}) collective-permute-start(bf16[512,1024]{1,0:T(8,128)(2,1)S(1)} %get-tuple-element.18), channel_id=1, source_target_pairs={{1,0},{2,1},{3,2},{4,3},{5,4},{6,5},{7,6},{8,7},{9,8},{10,9},{11,1... | collective-permute-start | bytes 3145736 | tf_op jit(solution)/shard_map/ppermute | solution.py:125
  177.0 71.5 %collective-permute-start.3 = (bf16[512,1024]{1,0:T(8,128)(2,1)}, bf16[512,1024]{1,0:T(8,128)(2,1)S(1)}, u32[]{:S(2)}, u32[]{:S(2)}) collective-permute-start(bf16[512,1024]{1,0:T(8,128)(2,1)} %get-tuple-element.16), channel_id=1, source_target_pairs={{1,0},{2,1},{3,2},{4,3},{5,4},{6,5},{7,6},{8,7},{9,8},{10,9},{11,1... | collective-permute-start | bytes 3145736 | tf_op jit(solution)/shard_map/ppermute | solution.py:125
Sparse Core Ops, SparseCore 0:
  10.8 51.7 all-gather.2
  65.4 41.9 all-gather.4
  169.5 75.8 reduce-scatter.2
  249.1 76.7 reduce-scatter.4
  331.3 155.1 all-reduce.2

commit v2 on v1

v2 whole, which is shorter than its diff:
```python
import jax
import jax.numpy as jnp
from jax import lax
from jax.experimental import pallas as pl
from jax.experimental.pallas import tpu as pltpu
from jax.sharding import PartitionSpec as P

F32 = jnp.float32
BF = jnp.bfloat16
NEG = -1e30
QB = 256
BAND = 512 + QB
PAIRS = 8
MESH = pl.DeviceIdType.MESH


def nt(a, b):
    return lax.dot_general(a, b, (((1,), (1,)), ((), ())), preferred_element_type=F32)


def nn(a, b):
    return lax.dot_general(a, b, (((1,), (0,)), ((), ())), preferred_element_type=F32)


def tn(a, b):
    return lax.dot_general(a, b, (((0,), (0,)), ((), ())), preferred_element_type=F32)


def cols(p):
    return pl.ds(pl.multiple_of(p * 128, 128), 128)


def part(index, size):
    return pl.ds(pl.multiple_of(index * size, size), size)


def kernel(
    q_ref, k_ref, v_ref, cot_ref, w_ref, pick_ref, slots_ref, blocks_ref, fill_ref,
    dq_ref, dk_ref, dv_ref, wg_ref,
    kx, vx, dkt, dvt, att, do_all, vcol, own,
    mem, halo, bsend, brecv, mg, srecv, xs, xrecv, ys, yrecv,
    wb, w1, ws2, w2, ws3, w3, ws4, w4, f5, f6, f7, f8,
    agy_s, agy_r, agx_s, agx_r, ags_s, ags_r, hal_s, hal_r, bak_s, bak_r,
    ms_s, ms_r, mx_s, mx_r, my_s, my_r,
    s1_s, s1_r, s2_s, s2_r, s3_s, s3_r, s4_s, s4_r, s5_s, s5_r, s6_s, s6_r, s7_s, s7_r, s8_s, s8_r,
):
    z = lax.axis_index("fam")
    me = lax.axis_index("ctx")
    x = me // 8
    y = (me // 2) % 4
    core = me % 2

    def at(xx, yy, cc):
        return (z, xx * 8 + yy * 2 + cc)

    sib = at(x, y, 1 - core)
    nxt = (z, (me + 1) % 32)
    prv = (z, (me + 31) % 32)
    across = (z, (me + 31 + 2 * core) % 32)
    ypeer = [at(x, (y + d) % 4, core) for d in (1, 2, 3)]
    xpeer = [at((x + d) % 4, y, core) for d in (1, 2, 3)]
    zpeer = [((z + d) % 4, me) for d in (1, 2, 3)]

    def rc(src, dst, send, recv, device):
        return pltpu.make_async_remote_copy(
            src_ref=src, dst_ref=dst, send_sem=send, recv_sem=recv, device_id=device, device_id_type=MESH
        )

    def ag_y():
        rows = part(core * 16 + x * 4 + y, 16)
        ref = mem.at[:, :, rows]
        return [rc(ref, ref, agy_s.at[d], agy_r.at[d], ypeer[d]) for d in range(3)]

    def ag_x(p):
        ref = mem.at[p, :, part(core * 4 + x, 64)]
        return [rc(ref, ref, agx_s.at[p, d], agx_r.at[p, d], xpeer[d]) for d in range(3)]

    def ag_s(p):
        ref = mem.at[p, :, part(core, 256)]
        return [rc(ref, ref, ags_s.at[p], ags_r.at[p], sib)]

    def halo_fwd(p):
        return [
            rc(r.at[:, cols(p)], halo.at[p, i], hal_s.at[p, i], hal_r.at[p, i], nxt)
            for i, r in enumerate((k_ref, v_ref))
        ]

    def halo_back(p):
        return [rc(bsend.at[p], brecv.at[p], bak_s.at[p], bak_r.at[p], prv)]

    def mem_s(p):
        return [rc(mg.at[p, :, part(1 - core, 256)], srecv.at[p], ms_s.at[p], ms_r.at[p], sib)]

    def mem_x(p):
        return [
            rc(xs.at[p, :, part((x + d + 1) % 4, 64)], xrecv.at[p, d], mx_s.at[p, d], mx_r.at[p, d], xpeer[d])
            for d in range(3)
        ]

    def mem_y(p):
        return [
            rc(ys.at[p, :, part((y + d + 1) % 4, 16)], yrecv.at[p, d], my_s.at[p, d], my_r.at[p, d], ypeer[d])
            for d in range(3)
        ]

    def wt1(p):
        return [rc(wb.at[p, 1 - core], w1.at[p], s1_s.at[p], s1_r.at[p], sib)]

    def wt2(p):
        return [
            rc(ws2.at[p, part((z + d + 1) % 4, 32)], w2.at[p, d], s2_s.at[p, d], s2_r.at[p, d], zpeer[d])
            for d in range(3)
        ]

    def wt3(p):
        return [
            rc(ws3.at[p, (y + d + 1) % 4], w3.at[p, d], s3_s.at[p, d], s3_r.at[p, d], ypeer[d])
            for d in range(3)
        ]

    def wt4(p):
        return [
            rc(ws4.at[p, part((x + d + 1) % 4, 8)], w4.at[p, d], s4_s.at[p, d], s4_r.at[p, d], xpeer[d])
            for d in range(3)
        ]

    def wt5(p):
        ref = f5.at[p, part(x, 8)]
        return [rc(ref, ref, s5_s.at[p, d], s5_r.at[p, d], xpeer[d]) for d in range(3)]

    def wt6(p):
        ref = f6.at[p, y]
        return [rc(ref, ref, s6_s.at[p, d], s6_r.at[p, d], ypeer[d]) for d in range(3)]

    def wt7(p):
        ref = f7.at[p, part(z, 32)]
        return [rc(ref, ref, s7_s.at[p, d], s7_r.at[p, d], zpeer[d]) for d in range(3)]

    def wt8(p):
        return [rc(f7.at[p], f8.at[p], s8_s.at[p], s8_r.at[p], sib)]

    def start(copies):
        for c in copies:
            c.start()

    def wait(copies):
        for c in copies:
            c.wait()

    barrier = pltpu.get_barrier_semaphore()
    for device in [sib, across] + ypeer + xpeer + zpeer:
        pl.semaphore_signal(barrier, inc=1, device_id=device, device_id_type=MESH)
    mine = part(core * 16 + x * 4 + y, 16)
    pick = pick_ref[...]
    for i, r in enumerate((k_ref, v_ref)):
        for p in range(PAIRS):
            mem[p, i, mine, :] = nn(pick, r[:, p * 128 : p * 128 + 128]).astype(BF)
    pl.semaphore_wait(barrier, 11)
    start(ag_y())
    start(halo_fwd(0))
    start(halo_fwd(1))

    pos_band = me * 512 - 512 + lax.broadcasted_iota(jnp.int32, (1, 1024), 1)
    order = lax.broadcasted_iota(jnp.int32, (1, 512), 1) // 16
    holder = (order % 16) * 2 + order // 16
    pos = jnp.concatenate([pos_band, holder * 512 + slots_ref[...]], axis=1)
    block = (pos + 512) // 128 - 4
    prot = jnp.zeros((1, 1536), jnp.int32)
    limit = jnp.zeros((1, 1536), jnp.int32)
    first = jnp.int32(0)
    for i in range(32):
        size = blocks_ref[0, i]
        end = first + size
        inside = (block >= first) & (block < end)
        prot = jnp.where(inside, i, prot)
        limit = jnp.where(inside, (end - 1) * 128 + fill_ref[0, i], limit)
        first = end
    real = (pos >= 0) & (pos < limit)
    is_mem = lax.broadcasted_iota(jnp.int32, (1, 1536), 1) >= 1024
    rows8 = lax.broadcasted_iota(jnp.int32, (8, 1536), 0)
    table = jnp.where(rows8 == 4, jnp.where(real, 1.0, 0.0), 0.0)
    for a in range(4):
        mine_prot = prot[:, 512 + a * 128 : 513 + a * 128]
        seen = real & ((is_mem & (prot < mine_prot)) | (jnp.logical_not(is_mem) & (prot == mine_prot)))
        table = jnp.where(rows8 == a, jnp.where(seen, 0.0, NEG), table)
    wide = jnp.concatenate([table, jnp.zeros((120, 1536), F32)], axis=0).T
    kx[:, 128:] = wide.astype(BF)
    vcol[...] = wide[512:1024, :]
    vx[:, 128:] = jnp.where(lax.broadcasted_iota(jnp.int32, (1536, 128), 1) < 2, 1.0, 0.0).astype(BF)

    wait(ag_y())
    start(ag_x(0))
    start(ag_x(1))
    for p in range(PAIRS):
        do_all[p] = nt(cot_ref[...], w_ref[p * 128 : p * 128 + 128, :]).astype(BF)
    wait(ag_x(0))
    start(ag_s(0))

    lo = lax.broadcasted_iota(jnp.int32, (QB, 128), 1) < 64
    lane2 = lax.broadcasted_iota(jnp.int32, (2 * QB, 128), 1)

    def compute(p):
        kx[0:512, :128] = halo[p, 0]
        kx[512:1024, :128] = k_ref[:, cols(p)]
        kx[1024:1536, :128] = mem[p, 0]
        vx[0:512, :128] = halo[p, 1]
        vx[512:1024, :128] = v_ref[:, cols(p)]
        vx[1024:1536, :128] = mem[p, 1]
        dkt[...] = jnp.zeros_like(dkt)
        dvt[...] = jnp.zeros_like(dvt)
        row2 = lax.broadcasted_iota(jnp.int32, (2 * QB, 128), 0)
        rr = lax.broadcasted_iota(jnp.int32, (2 * QB, QB), 0)
        rr = jnp.where(rr >= QB, rr - QB, rr)
        cc = lax.broadcasted_iota(jnp.int32, (2 * QB, QB), 1)
        zero = jnp.zeros((QB, 128), BF)
        memory = slice(1024, 1536)
        for b in range(512 // QB):
            rows = slice(b * QB, (b + 1) * QB)
            band = slice(b * QB, b * QB + BAND)
            qp = q_ref[rows, cols(p)] * jnp.asarray(0.125, BF)
            qs = jnp.concatenate([jnp.where(lo, qp, zero), jnp.where(lo, zero, qp)], 0)
            r2 = jnp.where(row2 >= QB, row2 - QB, row2) + b * QB
            onehot = jnp.where(lane2 == r2 // 128, 1.0, 0.0).astype(BF)
            qa = jnp.concatenate([qs, onehot], 1)
            sb = nt(qa, kx[band, :])
            sm = nt(qa, kx[memory, :])
            far = jnp.where(cc > rr, sb[:, :QB], NEG)
            near = jnp.where(cc <= rr, sb[:, 512:], NEG)
            s = jnp.concatenate([far, sb[:, QB:512], near, sm], 1)
            m = jnp.max(s, axis=1, keepdims=True)
            e = jnp.exp(s - m).astype(BF)
            eb, em = e[:, :BAND], e[:, BAND:]
            o = nn(eb, vx[band, :]) + nn(em, vx[memory, :])
            live = vcol[rows, 4:5]
            live = jnp.concatenate([live, live], 0)
            inv = live / jnp.maximum(o[:, 128:129], 1.0)
            a = o[:, :128] * inv
            dop = do_all[p, rows, :]
            dos = jnp.concatenate([jnp.where(lo, dop, zero), jnp.where(lo, zero, dop)], 0)
            dosf = dos.astype(F32)
            rd = jnp.sum(a * dosf, axis=1, keepdims=True)
            high = rd.astype(BF).astype(F32)
            tail = jnp.where(lane2 == 0, -high, jnp.where(lane2 == 1, high - rd, 0.0)).astype(BF)
            da = jnp.concatenate([dos, tail], 1)
            dsb = (eb.astype(F32) * nt(da, vx[band, :])).astype(BF)
            dsm = (em.astype(F32) * nt(da, vx[memory, :])).astype(BF)
            dqs = (nn(dsb, kx[band, :128]) + nn(dsm, kx[memory, :128])) * (inv * 0.125)
            dq_ref[rows, cols(p)] = jnp.where(lo, dqs[:QB], dqs[QB:]).astype(BF)
            att[rows, :] = jnp.where(lo, a[:QB], a[QB:]).astype(BF)
            qn = (qs.astype(F32) * inv).astype(BF)
            don = (dosf * inv).astype(BF)
            dkt[:, band] += tn(qn, dsb)
            dkt[:, memory] += tn(qn, dsm)
            dvt[:, band] += tn(don, eb)
            dvt[:, memory] += tn(don, em)
        for i, t in enumerate((dkt, dvt)):
            mg[p, i] = t[:, 1024:].T.astype(BF)
            bsend[p, i] = t[:, :512].T.astype(BF)
            own[p, i] = t[:, 512:1024].T
        for h in range(2):
            wb[p, h] = tn(att[...], cot_ref[:, h * 512 : h * 512 + 512]).astype(BF)

    def mem_sum_s(p):
        wait(mem_s(p))
        both = mg[p, :, part(core, 256), :].astype(F32) + srecv[p].astype(F32)
        xs[p] = both.astype(BF)
        start(mem_x(p))

    def mem_sum_x(p):
        wait(mem_x(p))
        total = xs[p, :, part(x, 64), :].astype(F32)
        for d in range(3):
            total += xrecv[p, d].astype(F32)
        ys[p] = total.astype(BF)
        start(mem_y(p))

    def mem_sum_y(p):
        wait(mem_y(p))
        wait(halo_back(p))
        total = ys[p, :, part(y, 16), :].astype(F32)
        for d in range(3):
            total += yrecv[p, d].astype(F32)
        high = total.astype(BF)
        low = (total - high.astype(F32)).astype(BF)
        for i, ref in enumerate((dk_ref, dv_ref)):
            grad = own[p, i] + brecv[p, i].astype(F32)
            grad += tn(pick_ref[...], high[i]) + tn(pick_ref[...], low[i])
            ref[:, cols(p)] = grad.astype(BF)

    def w_sum1(p):
        wait(wt1(p))
        ws2[p] = (wb[p, core].astype(F32) + w1[p].astype(F32)).astype(BF)
        start(wt2(p))

    def w_sum2(p):
        wait(wt2(p))
        total = ws2[p, part(z, 32), :].astype(F32)
        for d in range(3):
            total += w2[p, d].astype(F32)
        for c in range(4):
            ws3[p, c] = total[:, c * 128 : c * 128 + 128].astype(BF)
        start(wt3(p))

    def w_sum3(p):
        wait(wt3(p))
        total = ws3[p, y].astype(F32)
        for d in range(3):
            total += w3[p, d].astype(F32)
        ws4[p] = total
        start(wt4(p))

    def w_sum4(p):
        wait(wt4(p))
        total = ws4[p, part(x, 8), :]
        for d in range(3):
            total += w4[p, d]
        f5[p, part(x, 8), :] = total * (65536.0 ** -0.5)
        start(wt5(p))

    def w_put5(p):
        wait(wt5(p))
        f6[p, y] = f5[p].astype(BF)
        start(wt6(p))

    def w_put6(p):
        wait(wt6(p))
        for c in range(4):
            f7[p, part(z, 32), c * 128 : c * 128 + 128] = f6[p, c]
        start(wt7(p))

    def w_put7(p):
        wait(wt7(p))
        start(wt8(p))

    def w_put8(p):
        wait(wt8(p))
        rows = part(p, 128)
        wg_ref[rows, part(core, 512)] = f7[p].astype(F32)
        wg_ref[rows, part(1 - core, 512)] = f8[p].astype(F32)

    lagged = [
        (1, [mem_sum_s, w_sum1]),
        (2, [mem_sum_x, w_sum2]),
        (3, [mem_sum_y, w_sum3]),
        (4, [w_sum4]),
        (5, [w_put5]),
        (6, [w_put6]),
        (7, [w_put7]),
        (8, [w_put8]),
    ]

    def step(t, carry):
        @pl.when(t < PAIRS - 2)
        def _():
            start(ag_x(t + 2))
            start(halo_fwd(t + 2))

        @pl.when(t < PAIRS - 1)
        def _():
            wait(ag_x(t + 1))
            start(ag_s(t + 1))

        @pl.when(t < PAIRS)
        def _():
            wait(ag_s(t))
            wait(halo_fwd(t))
            compute(t)
            start(mem_s(t))
            start(wt1(t))
            start(halo_back(t))

        for lag, stages in lagged:

            @pl.when((t >= lag) & (t < PAIRS + lag))
            def _(lag=lag, stages=stages):
                for stage in stages:
                    stage(t - lag)

        return carry

    lax.fori_loop(0, PAIRS + 8, step, 0)


def per_device(queries, key_rows, value_rows, cotangent, out_weight, prot_blocks, last_fill, memory_slots):
    slots = memory_slots[0]
    own = lax.dynamic_slice_in_dim(slots, lax.axis_index("ctx") * 16, 16)
    pick = (own[:, None] == jnp.arange(512, dtype=jnp.int32)[None, :]).astype(BF)
    order = slots.reshape(16, 2, 16).transpose(1, 0, 2).reshape(1, 512)
    vmem = pl.BlockSpec(memory_space=pltpu.VMEM)
    smem = pl.BlockSpec(memory_space=pltpu.SMEM)
    dma = pltpu.SemaphoreType.DMA
    row = jax.ShapeDtypeStruct((512, 1024), BF)

    def buf(*shape, dtype=BF):
        return pltpu.VMEM(shape, dtype)

    sems = [(3,), (PAIRS, 3), (PAIRS,), (PAIRS, 2), (PAIRS,)]
    sems += [(PAIRS,), (PAIRS, 3), (PAIRS, 3)]
    sems += [(PAIRS,)] + [(PAIRS, 3)] * 6 + [(PAIRS,)]
    dq, dk, dv, weight = pl.pallas_call(
        kernel,
        out_shape=[row, row, row, jax.ShapeDtypeStruct((1024, 1024), F32)],
        in_specs=[vmem] * 7 + [smem] * 2,
        out_specs=[vmem] * 4,
        scratch_shapes=[
            buf(1536, 256), buf(1536, 256), buf(128, 1536, dtype=F32), buf(128, 1536, dtype=F32),
            buf(512, 128), buf(PAIRS, 512, 128), buf(512, 128, dtype=F32), buf(PAIRS, 2, 512, 128, dtype=F32),
            buf(PAIRS, 2, 512, 128), buf(PAIRS, 2, 512, 128), buf(PAIRS, 2, 512, 128), buf(PAIRS, 2, 512, 128),
            buf(PAIRS, 2, 512, 128), buf(PAIRS, 2, 256, 128), buf(PAIRS, 2, 256, 128), buf(PAIRS, 3, 2, 64, 128),
            buf(PAIRS, 2, 64, 128), buf(PAIRS, 3, 2, 16, 128),
            buf(PAIRS, 2, 128, 512), buf(PAIRS, 128, 512), buf(PAIRS, 128, 512), buf(PAIRS, 3, 32, 512),
            buf(PAIRS, 4, 32, 128), buf(PAIRS, 3, 32, 128), buf(PAIRS, 32, 128, dtype=F32),
            buf(PAIRS, 3, 8, 128, dtype=F32), buf(PAIRS, 32, 128, dtype=F32), buf(PAIRS, 4, 32, 128),
            buf(PAIRS, 128, 512), buf(PAIRS, 128, 512),
        ]
        + [dma(s) for s in sems for _ in range(2)],
        compiler_params=pltpu.CompilerParams(
            collective_id=0, has_side_effects=True, vmem_limit_bytes=62 * 2**20
        ),
        name="fused",
    )(
        queries[0], key_rows[0], value_rows[0], cotangent[0], out_weight, pick, order,
        prot_blocks, last_fill,
    )
    return dq[None], dk[None], dv[None], weight


def solution(mesh):
    row = P("fam", "ctx", None)
    fam = P("fam", None)
    return jax.shard_map(
        per_device,
        mesh=mesh,
        in_specs=(row, row, row, row, P(), fam, fam, fam),
        out_specs=(row, row, row, P()),
        check_vma=False,
    )
```

time: 499 us -> 134 us (0.27)
  waiting for transfers between devices: 385 us -> 0 us
  Pallas kernels: 57.5 us -> 120 us
  between operations: 13.9 us -> 0.67 us
  other arithmetic: 15 us -> 2.02 us
  starting transfers between devices: 10.8 us -> 0 us
  matrix products: 10.5 us -> 0 us
  local copies, waits for them, and re-layouts: 5.46 us -> 11 us
    psum x1 -> x0, waiting for transfers between devices: 157 us -> none  [per_device(): weight = lax.psum(weight, ('fam', 'ctx')) * (4 * 16384) ** (-0.5)]
    reduce_scatter x2 -> x0, waiting for transfers between devices: 132 us -> none  [the longest x1 77.4 us: per_device(): lax.psum_scatter(dv[1024:].astype(BF), 'ctx', scatter_dimension=0, tiled=...]
    all_gather x2 -> x0, waiting for transfers between devices: 68.9 us -> none  [the longest x1 44.9 us: per_device(): mv = lax.all_gather(nn(pick, v).astype(BF), 'ctx', axis=0, tiled=True)]
    pallas_call x1, Pallas kernels: 57.5 us -> 120 us  [per_device(): pl.pallas_call(kernel, out_shape=[row, row, row, jax.ShapeDtypeStruct((10...]
    ppermute x4 -> x0, waiting for transfers between devices: 26.2 us -> none  [the longest x2 14.1 us: per_device(): hk, hv = lax.ppermute((k, v), 'ctx', ahead)]
    ppermute x4 -> x0, starting transfers between devices: 10.6 us -> none  [the longest x2 6.52 us: per_device(): hk, hv = lax.ppermute((k, v), 'ctx', ahead)]
    dot_general x4 -> x0, matrix products: 10.5 us -> none  [the longest x2 6.27 us: tn(): lax.dot_general(a, b, (((0,), (0,)), ((), ())), preferred_element_type=F32)]
    unnamed x4 -> x7, local copies, waits for them, and re-layouts: 0.01 us -> 9.46 us
  transfers between devices with their start and end apart: 9 -> 0, of which waited for: 8 -> 0; matrix products, arithmetic and copies ran while one was open for 4% -> 0% of each run, Pallas kernels for 0% -> 0%
where the time goes in v2:
time: 134 us
  Pallas kernels  120 us (90%)
  local copies, waits for them, and re-layouts  11 us (8%)
  other arithmetic  2.02 us (2%)
    pallas_call x1, Pallas kernels, per_device(): pl.pallas_call(kernel, out_shape=[row, row, row, jax.ShapeDtypeStruct((10...  120 us
    unnamed x7, local copies, waits for them, and re-layouts  9.46 us

profile of v2, /device:TPU:1, one launch (start us, length us, event | category | flops | bytes accessed | tf_op | source)
XLA Modules:
  0.0 133.9 jit_solution(1455678544278610866)
XLA Ops:
  0.6 0.7 dynamic-slice_bitcast_fusion
  1.4 0.5 broadcast.3
  1.9 1.3 %reduce.3 = s32[512]{0:T(512)S(1)} reduce(s32[1,512]{1,0:T(1,128)} %param.15, s32[]{:T(128)} %broadcast.3), dimensions={0}, to_apply=%param.15.reduce_sub_computation.3 | reduce | bytes 4100 | tf_op args[7]
  3.2 0.1 reshape_squeeze.3
  3.3 0.7 reshape.14.slots_ref
  4.0 0.7 fusion.pick_ref
  4.7 120.2 %fused.1 = (bf16[512,1024]{1,0:T(8,128)(2,1)}, bf16[512,1024]{1,0:T(8,128)(2,1)}, bf16[512,1024]{1,0:T(8,128)(2,1)}, f32[1024,1024]{1,0:T(8,128)}) custom-call(bf16[512,1024]{1,0:T(8,128)(2,1)} %bitcast.12, bf16[512,1024]{1,0:T(8,128)(2,1)} %bitcast.13, bf16[512,1024]{1,0:T(8,128)(2,1)} %bitcast.14, bf16[512,1024]{1,0:T(8,128)(2,1)} %bitcast.15, ...), custom_call_target="tpu_custom_call" | custom-call | tf_op jit(solution)/shard_map/fused/pallas_call | solution.py:400
  124.9 0.0 copy-start
  124.9 2.4 %copy.19 = bf16[1,512,1024]{2,1,0:T(8,128)(2,1)} copy(bf16[1,512,1024]{2,1,0:T(8,128)(2,1)} %bitcast.18) | data formatting | bytes 2097152
  127.3 2.3 %copy.20 = bf16[1,512,1024]{2,1,0:T(8,128)(2,1)} copy(bf16[1,512,1024]{2,1,0:T(8,128)(2,1)} %bitcast.17) | data formatting | bytes 2097152
  129.6 2.3 %copy.21 = bf16[1,512,1024]{2,1,0:T(8,128)(2,1)} copy(bf16[1,512,1024]{2,1,0:T(8,128)(2,1)} %bitcast.16) | data formatting | bytes 2097152
  131.8 0.0 copy-done
  131.8 2.0 %copy.22 = f32[1024,1024]{1,0:T(8,128)} copy(f32[1024,1024]{1,0:T(8,128)S(1)} %copy-done) | data formatting | bytes 8388608
  (1 shorter events, 0.0 us)
Async XLA Ops:
  124.9 7.0 %copy-start = (f32[1024,1024]{1,0:T(8,128)S(1)}, f32[1024,1024]{1,0:T(8,128)}, u32[]{:S(2)}) copy-start(f32[1024,1024]{1,0:T(8,128)} %get-tuple-element.19) | copy-start | bytes 12582916

commit v3 on v2

v3 whole, which is shorter than its diff:
```python
import jax
import jax.numpy as jnp
from jax import lax
from jax.experimental import pallas as pl
from jax.experimental.pallas import tpu as pltpu
from jax.sharding import PartitionSpec as P

F32 = jnp.float32
BF = jnp.bfloat16
NEG = -1e30
QB = 256
BAND = 512 + QB
PAIRS = 8
LEAD = 2
RING = LEAD + 1
MESH = pl.DeviceIdType.MESH


def nt(a, b):
    return lax.dot_general(a, b, (((1,), (1,)), ((), ())), preferred_element_type=F32)


def nn(a, b):
    return lax.dot_general(a, b, (((1,), (0,)), ((), ())), preferred_element_type=F32)


def tn(a, b):
    return lax.dot_general(a, b, (((0,), (0,)), ((), ())), preferred_element_type=F32)


def cols(p):
    return pl.ds(pl.multiple_of(p * 128, 128), 128)


def part(index, size):
    return pl.ds(pl.multiple_of(index * size, size), size)


def kernel(
    q_ref, k_ref, v_ref, cot_ref, w_ref, slots_ref, slot_ref, blocks_ref, fill_ref,
    dq_ref, dk_ref, dv_ref, wg_ref,
    kv, ebuf, inv_buf, rd_buf, bias, pick_ref, dkt, dvt, att, do_all, vcol, own,
    bsend, brecv, mg, srecv, xs, xrecv, ys, yrecv,
    wb, w1, ws2, w2, ws3, w3, ws4, w4, f5, f6, f7,
    agy_s, agy_r, agx_s, agx_r, ags_s, ags_r, hal_s, hal_r, bak_s, bak_r,
    ms_s, ms_r, mx_s, mx_r, my_s, my_r,
    s1_s, s1_r, s2_s, s2_r, s3_s, s3_r, s4_s, s4_r, s5_s, s5_r, s6_s, s6_r, s7_s, s7_r, s8_s, s8_r,
):
    z = lax.axis_index("fam")
    me = lax.axis_index("ctx")
    x = me // 8
    y = (me // 2) % 4
    core = me % 2

    def at(xx, yy, cc):
        return (z, xx * 8 + yy * 2 + cc)

    sib = at(x, y, 1 - core)
    nxt = (z, (me + 1) % 32)
    prv = (z, (me + 31) % 32)
    across = (z, (me + 31 + 2 * core) % 32)
    ypeer = [at(x, (y + d) % 4, core) for d in (1, 2, 3)]
    xpeer = [at((x + d) % 4, y, core) for d in (1, 2, 3)]
    zpeer = [((z + d) % 4, me) for d in (1, 2, 3)]

    def rc(src, dst, send, recv, device):
        return pltpu.make_async_remote_copy(
            src_ref=src, dst_ref=dst, send_sem=send, recv_sem=recv, device_id=device, device_id_type=MESH
        )

    def ag_y():
        ref = kv.at[:, :, part(64 + core * 16 + x * 4 + y, 16)]
        return [rc(ref, ref, agy_s.at[d], agy_r.at[d], ypeer[d]) for d in range(3)]

    def ag_x(p):
        ref = kv.at[p, :, part(16 + core * 4 + x, 64)]
        return [rc(ref, ref, agx_s.at[p, d], agx_r.at[p, d], xpeer[d]) for d in range(3)]

    def ag_s(p):
        ref = kv.at[p, :, part(4 + core, 256)]
        return [rc(ref, ref, ags_s.at[p], ags_r.at[p], sib)]

    def halo_fwd(p):
        return [rc(kv.at[p, :, 512:1024], kv.at[p, :, 0:512], hal_s.at[p], hal_r.at[p], nxt)]

    def halo_back(p):
        return [rc(bsend.at[p], brecv.at[p], bak_s.at[p], bak_r.at[p], prv)]

    def mem_s(p):
        return [rc(mg.at[p, :, part(1 - core, 256)], srecv.at[p], ms_s.at[p], ms_r.at[p], sib)]

    def mem_x(p):
        return [
            rc(xs.at[p, :, part((x + d + 1) % 4, 64)], xrecv.at[p, d], mx_s.at[p, d], mx_r.at[p, d], xpeer[d])
            for d in range(3)
        ]

    def mem_y(p):
        return [
            rc(ys.at[p, :, part((y + d + 1) % 4, 16)], yrecv.at[p, d], my_s.at[p, d], my_r.at[p, d], ypeer[d])
            for d in range(3)
        ]

    def wt1(p):
        return [rc(wb.at[p, 1 - core], w1.at[p], s1_s.at[p], s1_r.at[p], sib)]

    def wt2(p):
        return [
            rc(ws2.at[p, part((z + d + 1) % 4, 32)], w2.at[p, d], s2_s.at[p, d], s2_r.at[p, d], zpeer[d])
            for d in range(3)
        ]

    def wt3(p):
        return [
            rc(ws3.at[p, (y + d + 1) % 4], w3.at[p, d], s3_s.at[p, d], s3_r.at[p, d], ypeer[d])
            for d in range(3)
        ]

    def wt4(p):
        return [
            rc(ws4.at[p, part((x + d + 1) % 4, 8)], w4.at[p, d], s4_s.at[p, d], s4_r.at[p, d], xpeer[d])
            for d in range(3)
        ]

    def wt5(p):
        ref = f5.at[p, part(x, 8)]
        return [rc(ref, ref, s5_s.at[p, d], s5_r.at[p, d], xpeer[d]) for d in range(3)]

    def wt6(p):
        ref = f6.at[p, y]
        return [rc(ref, ref, s6_s.at[p, d], s6_r.at[p, d], ypeer[d]) for d in range(3)]

    def wt7(p):
        ref = f7.at[p, core, part(z, 32)]
        return [rc(ref, ref, s7_s.at[p, d], s7_r.at[p, d], zpeer[d]) for d in range(3)]

    def wt8(p):
        return [rc(f7.at[p, core], f7.at[p, core], s8_s.at[p], s8_r.at[p], sib)]

    def start(copies):
        for c in copies:
            c.start()

    def wait(copies):
        for c in copies:
            c.wait()

    barrier = pltpu.get_barrier_semaphore()
    for device in [sib, across] + ypeer + xpeer + zpeer:
        pl.semaphore_signal(barrier, inc=1, device_id=device, device_id_type=MESH)
    wide = lax.broadcasted_iota(jnp.int32, (16, 512), 1)
    line = lax.broadcasted_iota(jnp.int32, (16, 512), 0)
    chosen = jnp.zeros((16, 512), jnp.int32)
    for i in range(16):
        chosen = jnp.where(line == i, slot_ref[0, me * 16 + i], chosen)
    pick = jnp.where(wide == chosen, 1.0, 0.0).astype(BF)
    pick_ref[...] = pick
    mine = part(64 + core * 16 + x * 4 + y, 16)
    for i, r in enumerate((k_ref, v_ref)):
        for p in range(PAIRS):
            kv[p, i, 512:1024, :] = r[:, p * 128 : p * 128 + 128]
            kv[p, i, mine, :] = nn(pick, r[:, p * 128 : p * 128 + 128]).astype(BF)
    pl.semaphore_wait(barrier, 11)
    start(ag_y())
    start(halo_fwd(0))
    start(halo_fwd(1))

    here = lax.broadcasted_iota(jnp.int32, (512, 512), 1)
    there = lax.broadcasted_iota(jnp.int32, (512, 512), 0)
    origin = ((here // 16) % 16) * 32 + (here // 256) * 16 + here % 16
    move = jnp.where(there == origin, 1.0, 0.0).astype(BF)
    slots = jnp.broadcast_to(slots_ref[...], (16, 512))
    halves = nn((slots // 2).astype(F32).astype(BF), move)
    odds = nn((slots % 2).astype(F32).astype(BF), move)
    slots = (halves * 2.0 + odds).astype(jnp.int32)[:1]

    pos_band = me * 512 - 512 + lax.broadcasted_iota(jnp.int32, (1, 1024), 1)
    order = lax.broadcasted_iota(jnp.int32, (1, 512), 1) // 16
    holder = (order % 16) * 2 + order // 16
    pos = jnp.concatenate([pos_band, holder * 512 + slots], axis=1)
    block = (pos + 512) // 128 - 4
    prot = jnp.zeros((1, 1536), jnp.int32)
    limit = jnp.zeros((1, 1536), jnp.int32)
    first = jnp.int32(0)
    for i in range(32):
        end = first + blocks_ref[0, i]
        inside = (block >= first) & (block < end)
        prot = jnp.where(inside, i, prot)
        limit = jnp.where(inside, (end - 1) * 128 + fill_ref[0, i], limit)
        first = end
    real = (pos >= 0) & (pos < limit)
    is_mem = lax.broadcasted_iota(jnp.int32, (1, 1536), 1) >= 1024
    rows8 = lax.broadcasted_iota(jnp.int32, (8, 1536), 0)
    table = jnp.where(rows8 == 4, jnp.where(real, 1.0, 0.0), 0.0)
    for a in range(4):
        mine_prot = prot[:, 512 + a * 128 : 513 + a * 128]
        seen = real & ((is_mem & (prot < mine_prot)) | (jnp.logical_not(is_mem) & (prot == mine_prot)))
        table = jnp.where(rows8 == a, jnp.where(seen, 0.0, NEG), table)
    bias[...] = table
    vcol[...] = jnp.concatenate([table[:, 512:1024], jnp.zeros((120, 512), F32)], axis=0).T

    wait(ag_y())
    start(ag_x(0))
    start(ag_x(1))
    wait(ag_x(0))
    start(ag_s(0))

    lo = lax.broadcasted_iota(jnp.int32, (QB, 128), 1) < 64
    zero = jnp.zeros((QB, 128), BF)
    memory = slice(1024, 1536)

    def stacked(pair):
        return jnp.concatenate([jnp.where(lo, pair, zero), jnp.where(lo, zero, pair)], 0)

    def forward(p):
        slot = p % RING
        do_all[p] = nt(cot_ref[...], w_ref[part(p, 128), :]).astype(BF)
        rr = lax.broadcasted_iota(jnp.int32, (128, QB), 0)
        cc = lax.broadcasted_iota(jnp.int32, (128, QB), 1)
        for b in range(512 // QB):
            rows = slice(b * QB, (b + 1) * QB)
            band = slice(b * QB, b * QB + BAND)
            qs = stacked(q_ref[rows, cols(p)] * jnp.asarray(0.125, BF))
            sb = nt(qs, kv[p, 0, band, :])
            sm = nt(qs, kv[p, 0, memory, :])
            sums = []
            exps = []
            for g in range(2 * QB // 128):
                sub = g % (QB // 128)
                a = b * QB // 128 + sub
                group = slice(g * 128, g * 128 + 128)
                s = sb[group] + bias[a : a + 1, band]
                far = jnp.where(cc > rr + sub * 128, s[:, :QB], NEG)
                near = jnp.where(cc <= rr + sub * 128, s[:, 512:], NEG)
                s = jnp.concatenate([far, s[:, QB:512], near, sm[group] + bias[a : a + 1, memory]], 1)
                e = jnp.exp(s - jnp.max(s, axis=1, keepdims=True))
                sums.append(jnp.sum(e, axis=1, keepdims=True))
                exps.append(e.astype(BF))
            e = jnp.concatenate(exps, 0)
            ebuf[slot, b] = e
            o = nn(e[:, :BAND], kv[p, 1, band, :]) + nn(e[:, BAND:], kv[p, 1, memory, :])
            live = vcol[rows, 4:5]
            inv = jnp.concatenate([live, live], 0) / jnp.maximum(jnp.concatenate(sums, 0), 1.0)
            a = o * inv
            inv_buf[slot, b] = inv
            rd_buf[slot, b] = jnp.sum(a * stacked(do_all[p, rows, :]).astype(F32), axis=1, keepdims=True)
            att[rows, :] = jnp.where(lo, a[:QB], a[QB:]).astype(BF)
        for h in range(2):
            wb[p, h] = tn(att[...], cot_ref[:, h * 512 : h * 512 + 512]).astype(BF)

    def backward(p):
        slot = p % RING
        dkt[...] = jnp.zeros_like(dkt)
        dvt[...] = jnp.zeros_like(dvt)
        for b in range(512 // QB):
            rows = slice(b * QB, (b + 1) * QB)
            band = slice(b * QB, b * QB + BAND)
            inv = inv_buf[slot, b]
            rd = rd_buf[slot, b]
            dos = stacked(do_all[p, rows, :])
            eb = ebuf[slot, b, :, :BAND]
            em = ebuf[slot, b, :, BAND:]
            dsb = (eb.astype(F32) * (nt(dos, kv[p, 1, band, :]) - rd)).astype(BF)
            dsm = (em.astype(F32) * (nt(dos, kv[p, 1, memory, :]) - rd)).astype(BF)
            dqs = (nn(dsb, kv[p, 0, band, :]) + nn(dsm, kv[p, 0, memory, :])) * (inv * 0.125)
            dq_ref[rows, cols(p)] = jnp.where(lo, dqs[:QB], dqs[QB:]).astype(BF)
            qs = stacked(q_ref[rows, cols(p)] * jnp.asarray(0.125, BF))
            qn = (qs.astype(F32) * inv).astype(BF)
            don = (dos.astype(F32) * inv).astype(BF)
            dkt[:, band] += tn(qn, dsb)
            dkt[:, memory] += tn(qn, dsm)
            dvt[:, band] += tn(don, eb)
            dvt[:, memory] += tn(don, em)
        for i, t in enumerate((dkt, dvt)):
            mg[p, i] = t[:, 1024:].T.astype(BF)
            bsend[p, i] = t[:, :512].T.astype(BF)
            own[p, i] = t[:, 512:1024].T

    def mem_sum_s(p):
        wait(mem_s(p))
        both = mg[p, :, part(core, 256), :].astype(F32) + srecv[p].astype(F32)
        xs[p] = both.astype(BF)
        start(mem_x(p))

    def mem_sum_x(p):
        wait(mem_x(p))
        total = xs[p, :, part(x, 64), :].astype(F32)
        for d in range(3):
            total += xrecv[p, d].astype(F32)
        ys[p] = total.astype(BF)
        start(mem_y(p))

    def mem_sum_y(p):
        wait(mem_y(p))
        wait(halo_back(p))
        total = ys[p, :, part(y, 16), :].astype(F32)
        for d in range(3):
            total += yrecv[p, d].astype(F32)
        high = total.astype(BF)
        low = (total - high.astype(F32)).astype(BF)
        for i, ref in enumerate((dk_ref, dv_ref)):
            grad = own[p, i] + brecv[p, i].astype(F32)
            grad += tn(pick_ref[...], high[i]) + tn(pick_ref[...], low[i])
            ref[:, cols(p)] = grad.astype(BF)

    def w_sum1(p):
        wait(wt1(p))
        ws2[p] = (wb[p, core].astype(F32) + w1[p].astype(F32)).astype(BF)
        start(wt2(p))

    def w_sum2(p):
        wait(wt2(p))
        total = ws2[p, part(z, 32), :].astype(F32)
        for d in range(3):
            total += w2[p, d].astype(F32)
        for c in range(4):
            ws3[p, c] = total[:, c * 128 : c * 128 + 128].astype(BF)
        start(wt3(p))

    def w_sum3(p):
        wait(wt3(p))
        total = ws3[p, y].astype(F32)
        for d in range(3):
            total += w3[p, d].astype(F32)
        ws4[p] = total
        start(wt4(p))

    def w_sum4(p):
        wait(wt4(p))
        total = ws4[p, part(x, 8), :]
        for d in range(3):
            total += w4[p, d]
        f5[p, part(x, 8), :] = total * (65536.0 ** -0.5)
        start(wt5(p))

    def w_put5(p):
        wait(wt5(p))
        f6[p, y] = f5[p].astype(BF)
        start(wt6(p))

    def w_put6(p):
        wait(wt6(p))
        for c in range(4):
            f7[p, core, part(z, 32), c * 128 : c * 128 + 128] = f6[p, c]
        start(wt7(p))

    def w_put7(p):
        wait(wt7(p))
        start(wt8(p))

    def w_put8(p):
        wait(wt8(p))
        rows = part(p, 128)
        for h in range(2):
            wg_ref[rows, h * 512 : h * 512 + 512] = f7[p, h].astype(F32)

    between = [
        (1, w_sum2), (LEAD + 1, mem_sum_s), (2, w_sum4), (3, w_put6), (4, w_put8), (LEAD + 2, mem_sum_y),
    ]
    after = [(0, w_sum1), (1, w_sum3), (LEAD + 1, mem_sum_x), (2, w_put5), (3, w_put7)]

    def run(t, stages):
        for lag, stage in stages:

            @pl.when((t >= lag) & (t < PAIRS + lag))
            def _(lag=lag, stage=stage):
                stage(t - lag)

    def step(t, carry):
        @pl.when(t < PAIRS - 2)
        def _():
            start(ag_x(t + 2))
            start(halo_fwd(t + 2))

        @pl.when(t < PAIRS - 1)
        def _():
            wait(ag_x(t + 1))
            start(ag_s(t + 1))

        @pl.when(t < PAIRS)
        def _():
            wait(ag_s(t))
            wait(halo_fwd(t))
            forward(t)
            start(wt1(t))

        run(t, between)

        @pl.when((t >= LEAD) & (t < PAIRS + LEAD))
        def _():
            backward(t - LEAD)
            start(mem_s(t - LEAD))
            start(halo_back(t - LEAD))

        run(t, after)
        return carry

    lax.fori_loop(0, PAIRS + LEAD + 2, step, 0)


def handed_on(*refs):
    sources, targets, sems = refs[:4], refs[4:8], refs[8]
    copies = [pltpu.make_async_copy(a, b, sems.at[i]) for i, (a, b) in enumerate(zip(sources, targets))]
    for c in copies:
        c.start()
    for c in copies:
        c.wait()


def per_device(queries, key_rows, value_rows, cotangent, out_weight, prot_blocks, last_fill, memory_slots):
    vmem = pl.BlockSpec(memory_space=pltpu.VMEM)
    smem = pl.BlockSpec(memory_space=pltpu.SMEM)
    dma = pltpu.SemaphoreType.DMA
    row = jax.ShapeDtypeStruct((512, 1024), BF)

    def buf(*shape, dtype=BF):
        return pltpu.VMEM(shape, dtype)

    sems = [(3,), (PAIRS, 3), (PAIRS,), (PAIRS,), (PAIRS,)]
    sems += [(PAIRS,), (PAIRS, 3), (PAIRS, 3)]
    sems += [(PAIRS,)] + [(PAIRS, 3)] * 6 + [(PAIRS,)]
    shapes = [row, row, row, jax.ShapeDtypeStruct((1024, 1024), F32)]
    outs = pl.pallas_call(
        kernel,
        out_shape=shapes,
        in_specs=[vmem] * 6 + [smem] * 3,
        out_specs=[vmem] * 4,
        scratch_shapes=[
            buf(PAIRS, 2, 1536, 128), buf(RING, 512 // QB, 2 * QB, BAND + 512),
            buf(RING, 512 // QB, 2 * QB, 1, dtype=F32), buf(RING, 512 // QB, 2 * QB, 1, dtype=F32),
            buf(8, 1536, dtype=F32), buf(16, 512), buf(128, 1536, dtype=F32), buf(128, 1536, dtype=F32),
            buf(512, 128), buf(PAIRS, 512, 128), buf(512, 128, dtype=F32), buf(PAIRS, 2, 512, 128, dtype=F32),
            buf(PAIRS, 2, 512, 128), buf(PAIRS, 2, 512, 128),
            buf(PAIRS, 2, 512, 128), buf(PAIRS, 2, 256, 128), buf(PAIRS, 2, 256, 128), buf(PAIRS, 3, 2, 64, 128),
            buf(PAIRS, 2, 64, 128), buf(PAIRS, 3, 2, 16, 128),
            buf(PAIRS, 2, 128, 512), buf(PAIRS, 128, 512), buf(PAIRS, 128, 512), buf(PAIRS, 3, 32, 512),
            buf(PAIRS, 4, 32, 128), buf(PAIRS, 3, 32, 128), buf(PAIRS, 32, 128, dtype=F32),
            buf(PAIRS, 3, 8, 128, dtype=F32), buf(PAIRS, 32, 128, dtype=F32), buf(PAIRS, 4, 32, 128),
            buf(PAIRS, 2, 128, 512),
        ]
        + [dma(s) for s in sems for _ in range(2)],
        compiler_params=pltpu.CompilerParams(
            collective_id=0, has_side_effects=True, vmem_limit_bytes=62 * 2**20
        ),
        name="fused",
    )(
        queries[0], key_rows[0], value_rows[0], cotangent[0], out_weight, memory_slots,
        memory_slots, prot_blocks, last_fill,
    )
    hbm = pl.BlockSpec(memory_space=pl.ANY)
    dq, dk, dv, weight = pl.pallas_call(
        handed_on,
        out_shape=shapes,
        in_specs=[hbm] * 4,
        out_specs=[hbm] * 4,
        scratch_shapes=[dma((4,))],
        name="handed_on",
    )(*outs)
    return dq[None], dk[None], dv[None], weight


def solution(mesh):
    row = P("fam", "ctx", None)
    fam = P("fam", None)
    return jax.shard_map(
        per_device,
        mesh=mesh,
        in_specs=(row, row, row, row, P(), fam, fam, fam),
        out_specs=(row, row, row, P()),
        check_vma=False,
    )
```

time: 134 us -> 354 us (2.64)
  Pallas kernels: 120 us -> 353 us
  local copies, waits for them, and re-layouts: 11 us -> 0 us
    pallas_call x1 -> x2, Pallas kernels: 120 us -> 353 us  [the longest x1 223 us: per_device(): pl.pallas_call(handed_on, out_shape=shapes, in_specs=[hbm] * 4, out_specs...]
    unnamed x7 -> x0, local copies, waits for them, and re-layouts: 9.46 us -> none
where the time goes in v3:
time: 354 us
  Pallas kernels  353 us (100%)
    pallas_call x1, Pallas kernels, per_device(): pl.pallas_call(handed_on, out_shape=shapes, in_specs=[hbm] * 4, out_specs...  223 us
    pallas_call x1, Pallas kernels, per_device(): pl.pallas_call(kernel, out_shape=shapes, in_specs=[vmem] * 6 + [smem] * 3...  129 us

profile of v3, /device:TPU:1, one launch (start us, length us, event | category | flops | bytes accessed | tf_op | source)
XLA Modules:
  0.0 353.5 jit_solution(8252704056464190090)
XLA Ops:
  0.6 129.4 %fused.1 = (bf16[512,1024]{1,0:T(8,128)(2,1)}, bf16[512,1024]{1,0:T(8,128)(2,1)}, bf16[512,1024]{1,0:T(8,128)(2,1)}, f32[1024,1024]{1,0:T(8,128)}) custom-call(bf16[512,1024]{1,0:T(8,128)(2,1)} %bitcast.7, bf16[512,1024]{1,0:T(8,128)(2,1)} %bitcast.8, bf16[512,1024]{1,0:T(8,128)(2,1)} %bitcast.9, bf16[512,1024]{1,0:T(8,128)(2,1)} %bitcast.10, ...), custom_call_target="tpu_custom_call" | custom-call | tf_op jit(solution)/shard_map/fused/pallas_call | solution.py:423
  130.1 223.5 %handed_on.1 = (bf16[512,1024]{1,0:T(8,128)(2,1)}, bf16[512,1024]{1,0:T(8,128)(2,1)}, bf16[512,1024]{1,0:T(8,128)(2,1)}, f32[1024,1024]{1,0:T(8,128)}) custom-call(bf16[512,1024]{1,0:T(8,128)(2,1)} %get-tuple-element.12.refs_0_, bf16[512,1024]{1,0:T(8,128)(2,1)} %get-tuple-element.13.refs_1_, bf16[512,1024]{1,0:T(8,128)(2,1)} %get-tuple-element.14.refs_2_, ...), custom_call_target="tpu_custom_call" | custom-call | tf_op jit(solution)/shard_map/handed_on/pallas_call | solution.py:451

commit v4 on v3

--- a/solution.py
+++ b/solution.py
@@ -91,7 +91,7 @@
 
     def mem_x(p):
         return [
-            rc(xs.at[p, :, part((x + d + 1) % 4, 64)], xrecv.at[p, d], mx_s.at[p, d], mx_r.at[p, d], xpeer[d])
+            rc(xs.at[p, :, part((x + 3 - d) % 4, 64)], xrecv.at[p, d], mx_s.at[p, d], mx_r.at[p, d], xpeer[2 - d])
             for d in range(3)
         ]
 
@@ -144,6 +144,48 @@
     def wait(copies):
         for c in copies:
             c.wait()
+
+    def start_up(copies):
+        for d, c in enumerate(copies):
+            pl.when(x + d + 1 < 4)(c.start)
+
+    def wait_up(copies):
+        for d, c in enumerate(copies):
+            pl.when(x + d + 1 < 4)(c.wait_send)
+            pl.when(x >= d + 1)(c.wait_recv)
+
+    def start_down(copies):
+        for d, c in enumerate(copies):
+            pl.when(x >= d + 1)(c.start)
+
+    def wait_down(copies):
+        for d, c in enumerate(copies):
+            pl.when(x >= d + 1)(c.wait_send)
+            pl.when(x + d + 1 < 4)(c.wait_recv)
+
+    def start_fwd(p):
+        pl.when(me < 31)(halo_fwd(p)[0].start)
+
+    def wait_fwd(p):
+        pl.when(me < 31)(halo_fwd(p)[0].wait_send)
+        pl.when(me > 0)(halo_fwd(p)[0].wait_recv)
+
+    def start_back(p):
+        pl.when(me > 0)(halo_back(p)[0].start)
+
+    def wait_back(p):
+        pl.when(me > 0)(halo_back(p)[0].wait_send)
+        pl.when(me < 31)(halo_back(p)[0].wait_recv)
+
+    for p in range(PAIRS):
+        kv[p, :, 0:512, :] = jnp.zeros((2, 512, 128), BF)
+        kv[p, :, 1024:1536, :] = jnp.zeros((2, 512, 128), BF)
+        xrecv[p] = jnp.zeros((3, 2, 64, 128), BF)
+
+    @pl.when(me == 31)
+    def _():
+        for p in range(PAIRS):
+            brecv[p] = jnp.zeros((2, 512, 128), BF)
 
     barrier = pltpu.get_barrier_semaphore()
     for device in [sib, across] + ypeer + xpeer + zpeer:
@@ -162,8 +204,8 @@
             kv[p, i, mine, :] = nn(pick, r[:, p * 128 : p * 128 + 128]).astype(BF)
     pl.semaphore_wait(barrier, 11)
     start(ag_y())
-    start(halo_fwd(0))
-    start(halo_fwd(1))
+    start_fwd(0)
+    start_fwd(1)
 
     here = lax.broadcasted_iota(jnp.int32, (512, 512), 1)
     there = lax.broadcasted_iota(jnp.int32, (512, 512), 0)
@@ -200,9 +242,9 @@
     vcol[...] = jnp.concatenate([table[:, 512:1024], jnp.zeros((120, 512), F32)], axis=0).T
 
     wait(ag_y())
-    start(ag_x(0))
-    start(ag_x(1))
-    wait(ag_x(0))
+    start_up(ag_x(0))
+    start_up(ag_x(1))
+    wait_up(ag_x(0))
     start(ag_s(0))
 
     lo = lax.broadcasted_iota(jnp.int32, (QB, 128), 1) < 64
@@ -280,10 +322,10 @@
         wait(mem_s(p))
         both = mg[p, :, part(core, 256), :].astype(F32) + srecv[p].astype(F32)
         xs[p] = both.astype(BF)
-        start(mem_x(p))
+        start_down(mem_x(p))
 
     def mem_sum_x(p):
-        wait(mem_x(p))
+        wait_down(mem_x(p))
         total = xs[p, :, part(x, 64), :].astype(F32)
         for d in range(3):
             total += xrecv[p, d].astype(F32)
@@ -292,7 +334,7 @@
 
     def mem_sum_y(p):
         wait(mem_y(p))
-        wait(halo_back(p))
+        wait_back(p)
         total = ys[p, :, part(y, 16), :].astype(F32)
         for d in range(3):
             total += yrecv[p, d].astype(F32)
@@ -352,7 +394,7 @@
         wait(wt8(p))
         rows = part(p, 128)
         for h in range(2):
-            wg_ref[rows, h * 512 : h * 512 + 512] = f7[p, h].astype(F32)
+            wg_ref[rows, h * 512 : h * 512 + 512] = f7[p, h]
 
     between = [
         (1, w_sum2), (LEAD + 1, mem_sum_s), (2, w_sum4), (3, w_put6), (4, w_put8), (LEAD + 2, mem_sum_y),
@@ -369,18 +411,18 @@
     def step(t, carry):
         @pl.when(t < PAIRS - 2)
         def _():
-            start(ag_x(t + 2))
-            start(halo_fwd(t + 2))
+            start_up(ag_x(t + 2))
+            start_fwd(t + 2)
 
         @pl.when(t < PAIRS - 1)
         def _():
-            wait(ag_x(t + 1))
+            wait_up(ag_x(t + 1))
             start(ag_s(t + 1))
 
         @pl.when(t < PAIRS)
         def _():
             wait(ag_s(t))
-            wait(halo_fwd(t))
+            wait_fwd(t)
             forward(t)
             start(wt1(t))
 
@@ -390,7 +432,7 @@
         def _():
             backward(t - LEAD)
             start(mem_s(t - LEAD))
-            start(halo_back(t - LEAD))
+            start_back(t - LEAD)
 
         run(t, after)
         return carry
@@ -399,12 +441,8 @@
 
 
 def handed_on(*refs):
-    sources, targets, sems = refs[:4], refs[4:8], refs[8]
-    copies = [pltpu.make_async_copy(a, b, sems.at[i]) for i, (a, b) in enumerate(zip(sources, targets))]
-    for c in copies:
-        c.start()
-    for c in copies:
-        c.wait()
+    for source, target in zip(refs[:4], refs[4:]):
+        target[...] = source[...].astype(target.dtype)
 
 
 def per_device(queries, key_rows, value_rows, cotangent, out_weight, prot_blocks, last_fill, memory_slots):
@@ -419,10 +457,10 @@
     sems = [(3,), (PAIRS, 3), (PAIRS,), (PAIRS,), (PAIRS,)]
     sems += [(PAIRS,), (PAIRS, 3), (PAIRS, 3)]
     sems += [(PAIRS,)] + [(PAIRS, 3)] * 6 + [(PAIRS,)]
-    shapes = [row, row, row, jax.ShapeDtypeStruct((1024, 1024), F32)]
+    square = (1024, 1024)
     outs = pl.pallas_call(
         kernel,
-        out_shape=shapes,
+        out_shape=[row, row, row, jax.ShapeDtypeStruct(square, BF)],
         in_specs=[vmem] * 6 + [smem] * 3,
         out_specs=[vmem] * 4,
         scratch_shapes=[
@@ -447,13 +485,14 @@
         queries[0], key_rows[0], value_rows[0], cotangent[0], out_weight, memory_slots,
         memory_slots, prot_blocks, last_fill,
     )
-    hbm = pl.BlockSpec(memory_space=pl.ANY)
+    blocks = [pl.BlockSpec((128, 1024), lambda i: (i, 0))] * 3 + [pl.BlockSpec((256, 1024), lambda i: (i, 0))]
     dq, dk, dv, weight = pl.pallas_call(
         handed_on,
-        out_shape=shapes,
-        in_specs=[hbm] * 4,
-        out_specs=[hbm] * 4,
-        scratch_shapes=[dma((4,))],
+        grid=(4,),
+        out_shape=[row, row, row, jax.ShapeDtypeStruct(square, F32)],
+        in_specs=blocks,
+        out_specs=blocks,
+        compiler_params=pltpu.CompilerParams(vmem_limit_bytes=16 * 2**20),
         name="handed_on",
     )(*outs)
     return dq[None], dk[None], dv[None], weight

time: 354 us -> 137 us (0.39)
  Pallas kernels: 353 us -> 131 us
  local copies, waits for them, and re-layouts: 0 us -> 5.26 us
    pallas_call x2, Pallas kernels: 353 us -> 131 us  [the longest x1 127 us: per_device(): pl.pallas_call(kernel, out_shape=[row, row, row, jax.ShapeDtypeStruct(squ...]
    unnamed x0 -> x8, local copies, waits for them, and re-layouts: none -> 5.26 us
where the time goes in v4:
time: 137 us
  Pallas kernels  131 us (96%)
  local copies, waits for them, and re-layouts  5.26 us (4%)
    pallas_call x1, Pallas kernels, per_device(): pl.pallas_call(kernel, out_shape=[row, row, row, jax.ShapeDtypeStruct(squ...  127 us
    unnamed x8, local copies, waits for them, and re-layouts  5.26 us
    pallas_call x1, Pallas kernels, per_device(): pl.pallas_call(handed_on, grid=(4,), out_shape=[row, row, row, jax.ShapeD...  3.23 us

profile of v4, /device:TPU:1, one launch (start us, length us, event | category | flops | bytes accessed | tf_op | source)
XLA Modules:
  0.0 136.6 jit_solution(15735778045344082058)
XLA Ops:
  0.6 127.5 %fused.1 = (bf16[512,1024]{1,0:T(8,128)(2,1)}, bf16[512,1024]{1,0:T(8,128)(2,1)}, bf16[512,1024]{1,0:T(8,128)(2,1)}, bf16[1024,1024]{1,0:T(8,128)(2,1)}) custom-call(bf16[512,1024]{1,0:T(8,128)(2,1)} %bitcast.7, bf16[512,1024]{1,0:T(8,128)(2,1)} %bitcast.8, bf16[512,1024]{1,0:T(8,128)(2,1)} %bitcast.9, bf16[512,1024]{1,0:T(8,128)(2,1)} %bitcast.10, ...), custom_call_target="tpu_custom_call" | custom-call | tf_op jit(solution)/shard_map/fused/pallas_call | solution.py:461
  128.1 0.0 copy-start
  128.1 1.6 %copy-done = bf16[1024,1024]{1,0:T(8,128)(2,1)S(1)} copy-done((bf16[1024,1024]{1,0:T(8,128)(2,1)S(1)}, bf16[1024,1024]{1,0:T(8,128)(2,1)}, u32[]{:S(2)}) %copy-start) | copy-done | bytes 2097176
  129.7 0.0 copy-start.1
  129.7 1.2 copy-done.1
  130.9 0.0 copy-start.2
  130.9 1.2 copy-done.2
  132.1 0.0 copy-start.3
  132.2 1.2 copy-done.3
  133.4 3.2 %handed_on.1 = (bf16[512,1024]{1,0:T(8,128)(2,1)}, bf16[512,1024]{1,0:T(8,128)(2,1)}, bf16[512,1024]{1,0:T(8,128)(2,1)}, f32[1024,1024]{1,0:T(8,128)}) custom-call(bf16[512,1024]{1,0:T(8,128)(2,1)S(1)} %copy-done.1, bf16[512,1024]{1,0:T(8,128)(2,1)S(1)} %copy-done.2, bf16[512,1024]{1,0:T(8,128)(2,1)S(1)} %copy-done.3, bf16[1024,1024]{1,0:T(8,128)(2,1)S(1)} %copy-done), custom_call_target="tpu_custom_call" | custom-call | tf_op jit(solution)/shard_map/handed_on/pallas_call | solution.py:489
Async XLA Ops:
  128.1 1.6 %copy-start = (bf16[1024,1024]{1,0:T(8,128)(2,1)S(1)}, bf16[1024,1024]{1,0:T(8,128)(2,1)}, u32[]{:S(2)}) copy-start(bf16[1024,1024]{1,0:T(8,128)(2,1)} %get-tuple-element.15.refs_3_) | copy-start | bytes 6291460
  129.7 1.2 copy-start.1
  130.9 1.2 copy-start.2
  132.1 1.2 copy-start.3

commit v5 on v4

--- a/solution.py
+++ b/solution.py
@@ -11,8 +11,9 @@
 QB = 256
 BAND = 512 + QB
 PAIRS = 8
-LEAD = 2
+LEAD = 4
 RING = LEAD + 1
+KEEP = 3
 MESH = pl.DeviceIdType.MESH
 
 
@@ -39,7 +40,7 @@
 def kernel(
     q_ref, k_ref, v_ref, cot_ref, w_ref, slots_ref, slot_ref, blocks_ref, fill_ref,
     dq_ref, dk_ref, dv_ref, wg_ref,
-    kv, ebuf, inv_buf, rd_buf, bias, pick_ref, dkt, dvt, att, do_all, vcol, own,
+    kv, ebuf, stat, bias, pick_ref, dkt, dvt, att, do_all, vcol, own,
     bsend, brecv, mg, srecv, xs, xrecv, ys, yrecv,
     wb, w1, ws2, w2, ws3, w3, ws4, w4, f5, f6, f7,
     agy_s, agy_r, agx_s, agx_r, ags_s, ags_r, hal_s, hal_r, bak_s, bak_r,
@@ -284,8 +285,8 @@
             live = vcol[rows, 4:5]
             inv = jnp.concatenate([live, live], 0) / jnp.maximum(jnp.concatenate(sums, 0), 1.0)
             a = o * inv
-            inv_buf[slot, b] = inv
-            rd_buf[slot, b] = jnp.sum(a * stacked(do_all[p, rows, :]).astype(F32), axis=1, keepdims=True)
+            stat[slot, b, :, 0:1] = inv
+            stat[slot, b, :, 1:2] = jnp.sum(a * stacked(do_all[p, rows, :]).astype(F32), axis=1, keepdims=True)
             att[rows, :] = jnp.where(lo, a[:QB], a[QB:]).astype(BF)
         for h in range(2):
             wb[p, h] = tn(att[...], cot_ref[:, h * 512 : h * 512 + 512]).astype(BF)
@@ -297,8 +298,8 @@
         for b in range(512 // QB):
             rows = slice(b * QB, (b + 1) * QB)
             band = slice(b * QB, b * QB + BAND)
-            inv = inv_buf[slot, b]
-            rd = rd_buf[slot, b]
+            inv = stat[slot, b, :, 0:1]
+            rd = stat[slot, b, :, 1:2]
             dos = stacked(do_all[p, rows, :])
             eb = ebuf[slot, b, :, :BAND]
             em = ebuf[slot, b, :, BAND:]
@@ -316,7 +317,7 @@
         for i, t in enumerate((dkt, dvt)):
             mg[p, i] = t[:, 1024:].T.astype(BF)
             bsend[p, i] = t[:, :512].T.astype(BF)
-            own[p, i] = t[:, 512:1024].T
+            own[p % KEEP, i] = t[:, 512:1024].T
 
     def mem_sum_s(p):
         wait(mem_s(p))
@@ -341,7 +342,7 @@
         high = total.astype(BF)
         low = (total - high.astype(F32)).astype(BF)
         for i, ref in enumerate((dk_ref, dv_ref)):
-            grad = own[p, i] + brecv[p, i].astype(F32)
+            grad = own[p % KEEP, i] + brecv[p, i].astype(F32)
             grad += tn(pick_ref[...], high[i]) + tn(pick_ref[...], low[i])
             ref[:, cols(p)] = grad.astype(BF)
 
@@ -396,10 +397,11 @@
         for h in range(2):
             wg_ref[rows, h * 512 : h * 512 + 512] = f7[p, h]
 
-    between = [
-        (1, w_sum2), (LEAD + 1, mem_sum_s), (2, w_sum4), (3, w_put6), (4, w_put8), (LEAD + 2, mem_sum_y),
+    between = [(LEAD + 1, mem_sum_s), (7, w_put8)]
+    after = [
+        (LEAD + 1, mem_sum_x), (0, w_sum1), (1, w_sum2), (2, w_sum3), (3, w_sum4), (4, w_put5), (5, w_put6), (6, w_put7),
+        (LEAD + 2, mem_sum_y),
     ]
-    after = [(0, w_sum1), (1, w_sum3), (LEAD + 1, mem_sum_x), (2, w_put5), (3, w_put7)]
 
     def run(t, stages):
         for lag, stage in stages:
@@ -437,7 +439,7 @@
         run(t, after)
         return carry
 
-    lax.fori_loop(0, PAIRS + LEAD + 2, step, 0)
+    lax.fori_loop(0, PAIRS + max(LEAD + 2, 7), step, 0)
 
 
 def handed_on(*refs):
@@ -465,9 +467,9 @@
         out_specs=[vmem] * 4,
         scratch_shapes=[
             buf(PAIRS, 2, 1536, 128), buf(RING, 512 // QB, 2 * QB, BAND + 512),
-            buf(RING, 512 // QB, 2 * QB, 1, dtype=F32), buf(RING, 512 // QB, 2 * QB, 1, dtype=F32),
+            buf(RING, 512 // QB, 2 * QB, 128, dtype=F32),
             buf(8, 1536, dtype=F32), buf(16, 512), buf(128, 1536, dtype=F32), buf(128, 1536, dtype=F32),
-            buf(512, 128), buf(PAIRS, 512, 128), buf(512, 128, dtype=F32), buf(PAIRS, 2, 512, 128, dtype=F32),
+            buf(512, 128), buf(PAIRS, 512, 128), buf(512, 128, dtype=F32), buf(KEEP, 2, 512, 128, dtype=F32),
             buf(PAIRS, 2, 512, 128), buf(PAIRS, 2, 512, 128),
             buf(PAIRS, 2, 512, 128), buf(PAIRS, 2, 256, 128), buf(PAIRS, 2, 256, 128), buf(PAIRS, 3, 2, 64, 128),
             buf(PAIRS, 2, 64, 128), buf(PAIRS, 3, 2, 16, 128),
@@ -492,7 +494,7 @@
         out_shape=[row, row, row, jax.ShapeDtypeStruct(square, F32)],
         in_specs=blocks,
         out_specs=blocks,
-        compiler_params=pltpu.CompilerParams(vmem_limit_bytes=16 * 2**20),
+        compiler_params=pltpu.CompilerParams(vmem_limit_bytes=60 * 2**20),
         name="handed_on",
     )(*outs)
     return dq[None], dk[None], dv[None], weight

time: 137 us -> 120 us (0.88)
  Pallas kernels: 131 us -> 120 us
  local copies, waits for them, and re-layouts: 5.26 us -> 0 us
    pallas_call x1, Pallas kernels: 127 us -> 114 us  [per_device(): pl.pallas_call(kernel, out_shape=[row, row, row, jax.ShapeDtypeStruct(squ...]
    unnamed x8 -> x0, local copies, waits for them, and re-layouts: 5.26 us -> none
    pallas_call x1, Pallas kernels: 3.23 us -> 5.78 us  [per_device(): pl.pallas_call(handed_on, grid=(4,), out_shape=[row, row, row, jax.ShapeD...]
where the time goes in v5:
time: 120 us
  Pallas kernels  120 us (100%)
    pallas_call x1, Pallas kernels, per_device(): pl.pallas_call(kernel, out_shape=[row, row, row, jax.ShapeDtypeStruct(squ...  114 us
    pallas_call x1, Pallas kernels, per_device(): pl.pallas_call(handed_on, grid=(4,), out_shape=[row, row, row, jax.ShapeD...  5.78 us

profile of v5, /device:TPU:1, one launch (start us, length us, event | category | flops | bytes accessed | tf_op | source)
XLA Modules:
  0.0 120.2 jit_solution(762051997772359448)
XLA Ops:
  0.6 113.8 %fused.1 = (bf16[512,1024]{1,0:T(8,128)(2,1)}, bf16[512,1024]{1,0:T(8,128)(2,1)}, bf16[512,1024]{1,0:T(8,128)(2,1)}, bf16[1024,1024]{1,0:T(8,128)(2,1)}) custom-call(bf16[512,1024]{1,0:T(8,128)(2,1)} %bitcast.7, bf16[512,1024]{1,0:T(8,128)(2,1)} %bitcast.8, bf16[512,1024]{1,0:T(8,128)(2,1)} %bitcast.9, bf16[512,1024]{1,0:T(8,128)(2,1)} %bitcast.10, ...), custom_call_target="tpu_custom_call" | custom-call | tf_op jit(solution)/shard_map/fused/pallas_call | solution.py:463
  114.4 5.8 %handed_on.1 = (bf16[512,1024]{1,0:T(8,128)(2,1)}, bf16[512,1024]{1,0:T(8,128)(2,1)}, bf16[512,1024]{1,0:T(8,128)(2,1)}, f32[1024,1024]{1,0:T(8,128)}) custom-call(bf16[512,1024]{1,0:T(8,128)(2,1)} %get-tuple-element.12.refs_0_, bf16[512,1024]{1,0:T(8,128)(2,1)} %get-tuple-element.13.refs_1_, bf16[512,1024]{1,0:T(8,128)(2,1)} %get-tuple-element.14.refs_2_, ...), custom_call_target="tpu_custom_call" | custom-call | tf_op jit(solution)/shard_map/handed_on/pallas_call | solution.py:491

commit v6 on v5

--- a/solution.py
+++ b/solution.py
@@ -11,7 +11,7 @@
 QB = 256
 BAND = 512 + QB
 PAIRS = 8
-LEAD = 4
+LEAD = 2
 RING = LEAD + 1
 KEEP = 3
 MESH = pl.DeviceIdType.MESH
@@ -179,9 +179,13 @@
         pl.when(me < 31)(halo_back(p)[0].wait_recv)
 
     for p in range(PAIRS):
-        kv[p, :, 0:512, :] = jnp.zeros((2, 512, 128), BF)
         kv[p, :, 1024:1536, :] = jnp.zeros((2, 512, 128), BF)
         xrecv[p] = jnp.zeros((3, 2, 64, 128), BF)
+
+    @pl.when(me == 0)
+    def _():
+        for p in range(PAIRS):
+            kv[p, :, 0:512, :] = jnp.zeros((2, 512, 128), BF)
 
     @pl.when(me == 31)
     def _():
@@ -200,11 +204,14 @@
     pick_ref[...] = pick
     mine = part(64 + core * 16 + x * 4 + y, 16)
     for i, r in enumerate((k_ref, v_ref)):
+        chosen_rows = nn(pick, r[...]).astype(BF)
+        for p in range(PAIRS):
+            kv[p, i, mine, :] = chosen_rows[:, p * 128 : p * 128 + 128]
+    pl.semaphore_wait(barrier, 11)
+    start(ag_y())
+    for i, r in enumerate((k_ref, v_ref)):
         for p in range(PAIRS):
             kv[p, i, 512:1024, :] = r[:, p * 128 : p * 128 + 128]
-            kv[p, i, mine, :] = nn(pick, r[:, p * 128 : p * 128 + 128]).astype(BF)
-    pl.semaphore_wait(barrier, 11)
-    start(ag_y())
     start_fwd(0)
     start_fwd(1)
 
@@ -245,6 +252,8 @@
     wait(ag_y())
     start_up(ag_x(0))
     start_up(ag_x(1))
+    for p in range(PAIRS):
+        do_all[p] = nt(cot_ref[...], w_ref[p * 128 : p * 128 + 128, :]).astype(BF)
     wait_up(ag_x(0))
     start(ag_s(0))
 
@@ -257,7 +266,6 @@
 
     def forward(p):
         slot = p % RING
-        do_all[p] = nt(cot_ref[...], w_ref[part(p, 128), :]).astype(BF)
         rr = lax.broadcasted_iota(jnp.int32, (128, QB), 0)
         cc = lax.broadcasted_iota(jnp.int32, (128, QB), 1)
         for b in range(512 // QB):

time: 120 us -> 118 us (0.983)
  Pallas kernels: 120 us -> 117 us
    pallas_call x1, Pallas kernels: 114 us -> 111 us  [per_device(): pl.pallas_call(kernel, out_shape=[row, row, row, jax.ShapeDtypeStruct(squ...]
where the time goes in v6:
time: 118 us; the launch traced here: 117 us
  Pallas kernels  117 us (99%)
    pallas_call x1, Pallas kernels, per_device(): pl.pallas_call(kernel, out_shape=[row, row, row, jax.ShapeDtypeStruct(squ...  111 us
    pallas_call x1, Pallas kernels, per_device(): pl.pallas_call(handed_on, grid=(4,), out_shape=[row, row, row, jax.ShapeD...  5.78 us

profile of v6, /device:TPU:1, one launch (start us, length us, event | category | flops | bytes accessed | tf_op | source)
XLA Modules:
  0.0 117.5 jit_solution(3551767218592604256)
XLA Ops:
  0.6 111.0 %fused.1 = (bf16[512,1024]{1,0:T(8,128)(2,1)}, bf16[512,1024]{1,0:T(8,128)(2,1)}, bf16[512,1024]{1,0:T(8,128)(2,1)}, bf16[1024,1024]{1,0:T(8,128)(2,1)}) custom-call(bf16[512,1024]{1,0:T(8,128)(2,1)} %bitcast.7, bf16[512,1024]{1,0:T(8,128)(2,1)} %bitcast.8, bf16[512,1024]{1,0:T(8,128)(2,1)} %bitcast.9, bf16[512,1024]{1,0:T(8,128)(2,1)} %bitcast.10, ...), custom_call_target="tpu_custom_call" | custom-call | tf_op jit(solution)/shard_map/fused/pallas_call | solution.py:471
  111.7 5.8 %handed_on.1 = (bf16[512,1024]{1,0:T(8,128)(2,1)}, bf16[512,1024]{1,0:T(8,128)(2,1)}, bf16[512,1024]{1,0:T(8,128)(2,1)}, f32[1024,1024]{1,0:T(8,128)}) custom-call(bf16[512,1024]{1,0:T(8,128)(2,1)} %get-tuple-element.12.refs_0_, bf16[512,1024]{1,0:T(8,128)(2,1)} %get-tuple-element.13.refs_1_, bf16[512,1024]{1,0:T(8,128)(2,1)} %get-tuple-element.14.refs_2_, ...), custom_call_target="tpu_custom_call" | custom-call | tf_op jit(solution)/shard_map/handed_on/pallas_call | solution.py:499

commit v7 on v6

--- a/solution.py
+++ b/solution.py
@@ -11,7 +11,7 @@
 QB = 256
 BAND = 512 + QB
 PAIRS = 8
-LEAD = 2
+LEAD = 3
 RING = LEAD + 1
 KEEP = 3
 MESH = pl.DeviceIdType.MESH

time: 118 us -> 116 us (0.983)
  Pallas kernels: 117 us -> 115 us
    pallas_call x1, Pallas kernels: 111 us -> 109 us  [per_device(): pl.pallas_call(kernel, out_shape=[row, row, row, jax.ShapeDtypeStruct(squ...]
where the time goes in v7:
time: 116 us
  Pallas kernels  115 us (99%)
    pallas_call x1, Pallas kernels, per_device(): pl.pallas_call(kernel, out_shape=[row, row, row, jax.ShapeDtypeStruct(squ...  109 us
    pallas_call x1, Pallas kernels, per_device(): pl.pallas_call(handed_on, grid=(4,), out_shape=[row, row, row, jax.ShapeD...  5.78 us

profile of v7, /device:TPU:1, one launch (start us, length us, event | category | flops | bytes accessed | tf_op | source)
XLA Modules:
  0.0 115.6 jit_solution(4067982183859456829)
XLA Ops:
  0.6 109.1 %fused.1 = (bf16[512,1024]{1,0:T(8,128)(2,1)}, bf16[512,1024]{1,0:T(8,128)(2,1)}, bf16[512,1024]{1,0:T(8,128)(2,1)}, bf16[1024,1024]{1,0:T(8,128)(2,1)}) custom-call(bf16[512,1024]{1,0:T(8,128)(2,1)} %bitcast.7, bf16[512,1024]{1,0:T(8,128)(2,1)} %bitcast.8, bf16[512,1024]{1,0:T(8,128)(2,1)} %bitcast.9, bf16[512,1024]{1,0:T(8,128)(2,1)} %bitcast.10, ...), custom_call_target="tpu_custom_call" | custom-call | tf_op jit(solution)/shard_map/fused/pallas_call | solution.py:471
  109.8 5.8 %handed_on.1 = (bf16[512,1024]{1,0:T(8,128)(2,1)}, bf16[512,1024]{1,0:T(8,128)(2,1)}, bf16[512,1024]{1,0:T(8,128)(2,1)}, f32[1024,1024]{1,0:T(8,128)}) custom-call(bf16[512,1024]{1,0:T(8,128)(2,1)} %get-tuple-element.12.refs_0_, bf16[512,1024]{1,0:T(8,128)(2,1)} %get-tuple-element.13.refs_1_, bf16[512,1024]{1,0:T(8,128)(2,1)} %get-tuple-element.14.refs_2_, ...), custom_call_target="tpu_custom_call" | custom-call | tf_op jit(solution)/shard_map/handed_on/pallas_call | solution.py:499

commit v8 on v7

--- a/solution.py
+++ b/solution.py
@@ -411,12 +411,23 @@
         (LEAD + 2, mem_sum_y),
     ]
 
+    hurried = [w_sum1, w_sum2, w_sum3, w_sum4, w_put5, w_put6, w_put7, w_put8]
+
     def run(t, stages):
         for lag, stage in stages:
 
-            @pl.when((t >= lag) & (t < PAIRS + lag))
+            early = stage in hurried
+            last = PAIRS - 1 if early else PAIRS
+
+            @pl.when((t >= lag) & (t < last + lag))
             def _(lag=lag, stage=stage):
                 stage(t - lag)
+
+            if early and lag > 0:
+
+                @pl.when(t == last + lag - 1)
+                def _(stage=stage):
+                    stage(PAIRS - 1)
 
     def step(t, carry):
         @pl.when(t < PAIRS - 2)
@@ -438,6 +449,10 @@
 
         run(t, between)
 
+        @pl.when(t == PAIRS - 1)
+        def _():
+            w_sum1(PAIRS - 1)
+
         @pl.when((t >= LEAD) & (t < PAIRS + LEAD))
         def _():
             backward(t - LEAD)
@@ -447,7 +462,7 @@
         run(t, after)
         return carry
 
-    lax.fori_loop(0, PAIRS + max(LEAD + 2, 7), step, 0)
+    lax.fori_loop(0, PAIRS + max(LEAD + 2, 6), step, 0)
 
 
 def handed_on(*refs):

time: 116 us -> 116 us (level)
  no operation moved by 1% of the time
where the time goes in v8:
time: 116 us
  Pallas kernels  115 us (99%)
    pallas_call x1, Pallas kernels, per_device(): pl.pallas_call(kernel, out_shape=[row, row, row, jax.ShapeDtypeStruct(squ...  110 us
    pallas_call x1, Pallas kernels, per_device(): pl.pallas_call(handed_on, grid=(4,), out_shape=[row, row, row, jax.ShapeD...  5.78 us

profile of v8, /device:TPU:1, one launch (start us, length us, event | category | flops | bytes accessed | tf_op | source)
XLA Modules:
  0.0 116.1 jit_solution(15891738184551338557)
XLA Ops:
  0.6 109.7 %fused.1 = (bf16[512,1024]{1,0:T(8,128)(2,1)}, bf16[512,1024]{1,0:T(8,128)(2,1)}, bf16[512,1024]{1,0:T(8,128)(2,1)}, bf16[1024,1024]{1,0:T(8,128)(2,1)}) custom-call(bf16[512,1024]{1,0:T(8,128)(2,1)} %bitcast.7, bf16[512,1024]{1,0:T(8,128)(2,1)} %bitcast.8, bf16[512,1024]{1,0:T(8,128)(2,1)} %bitcast.9, bf16[512,1024]{1,0:T(8,128)(2,1)} %bitcast.10, ...), custom_call_target="tpu_custom_call" | custom-call | tf_op jit(solution)/shard_map/fused/pallas_call | solution.py:486
  110.3 5.8 %handed_on.1 = (bf16[512,1024]{1,0:T(8,128)(2,1)}, bf16[512,1024]{1,0:T(8,128)(2,1)}, bf16[512,1024]{1,0:T(8,128)(2,1)}, f32[1024,1024]{1,0:T(8,128)}) custom-call(bf16[512,1024]{1,0:T(8,128)(2,1)} %get-tuple-element.12.refs_0_, bf16[512,1024]{1,0:T(8,128)(2,1)} %get-tuple-element.13.refs_1_, bf16[512,1024]{1,0:T(8,128)(2,1)} %get-tuple-element.14.refs_2_, ...), custom_call_target="tpu_custom_call" | custom-call | tf_op jit(solution)/shard_map/handed_on/pallas_call | solution.py:514
